TPU v7x, 512 devices: a whole 4x8x8 slice. The times are simulated.
512 devices in a mesh: narrow: 16 (over z, core), wide: 32 (over x, y).
Axes of the slice: x: 4, y: 8, z: 8, core: 2. Of those that a mesh axis runs over, the one named last changes fastest.
Arguments:
- activations: bfloat16 [131072, 8192], P(('narrow', 'wide')), may hold values from -24 to 24
- out_grads: bfloat16 [131072, 512], P(('narrow', 'wide')), may hold values from -6 to 6
Outputs:
- mean_grad: float32 [8192, 512], P(('narrow', 'wide'))
All inputs are finite; a program needn't handle non-finite values.
Results may differ from a plain program's by a relative error of at most 0.0065.
Values may be sent and summed in bfloat16 or wider, within the bound.
A program may use at most 128 MiB of HBM per device.

v0:
```python
import math

import jax
import jax.numpy as jnp
from jax import lax
from jax.sharding import PartitionSpec as P

BLOCK = 128


EPSILON = 1e-06


def hadamard(length):
    positions = jnp.arange(length, dtype=jnp.int32)
    shared_bits = positions[:, None] & positions[None, :]
    parity = jnp.zeros((length, length), jnp.int32)
    for shift_bit in range(length.bit_length() - 1):
        parity = parity + (shared_bits >> shift_bit & 1)
    return (1 - 2 * (parity % 2)).astype(jnp.float32) / math.sqrt(length)


def encode(values):
    largest = jnp.max(jnp.abs(values), axis=-2)
    scales = jnp.exp2(jnp.ceil(jnp.log2(largest + EPSILON)))
    encoded = (values / scales[..., None, :]).astype(jnp.bfloat16)
    return (encoded, scales.astype(jnp.bfloat16))


def per_device(activations, out_grads):
    model_width = activations.shape[1]
    columns = out_grads.shape[1]
    narrow_count = lax.axis_size("narrow")
    wide_count = lax.axis_size("wide")
    own_rows = model_width // narrow_count
    wide_rows = own_rows // wide_count
    block_count = own_rows // BLOCK
    rotation = hadamard(BLOCK)
    weight_grad = jnp.dot(activations.T, out_grads, preferred_element_type=jnp.float32)
    blocked = weight_grad.reshape(model_width // BLOCK, BLOCK, columns)
    rotated = jnp.einsum("ij,bjc->bic", rotation, blocked, precision=lax.Precision.HIGHEST)
    encoded, scales = encode(rotated)
    regroup_encoded = lax.all_to_all(
        encoded.reshape(model_width, columns), "narrow", split_axis=0, concat_axis=0, tiled=True
    )
    regroup_scales = lax.all_to_all(scales, "narrow", split_axis=0, concat_axis=0, tiled=True)
    piece_columns = regroup_encoded.shape[1]
    dequantized = regroup_encoded.reshape(narrow_count, block_count, BLOCK, piece_columns).astype(
        jnp.float32
    )
    dequantized = dequantized * regroup_scales.reshape(
        narrow_count, block_count, 1, piece_columns
    ).astype(jnp.float32)
    summed, summed_scales = encode(jnp.sum(dequantized, axis=0))
    summed, summed_scales = (summed.reshape(own_rows, piece_columns), summed_scales)
    scale_rows = min(BLOCK, wide_rows)
    spread = jnp.repeat(summed_scales, BLOCK // scale_rows, axis=0)
    received, received_scales = (
        lax.all_to_all(summed, "wide", split_axis=0, concat_axis=0, tiled=True),
        lax.all_to_all(spread, "wide", split_axis=0, concat_axis=0, tiled=True),
    )
    dequantized = received.reshape(wide_count, wide_rows // scale_rows, scale_rows, columns).astype(
        jnp.float32
    )
    dequantized = dequantized * received_scales.reshape(
        wide_count, wide_rows // scale_rows, 1, columns
    ).astype(jnp.float32)
    reduced = jnp.sum(dequantized, axis=0).reshape(wide_rows, columns)
    return reduced / (narrow_count * wide_count)


def solution(mesh):
    return jax.shard_map(
        per_device,
        mesh=mesh,
        in_specs=(P(("narrow", "wide"), None), P(("narrow", "wide"), None)),
        out_specs=P(("narrow", "wide"), None),
        check_vma=False,
    )
```

profile of v0, /device:TPU:8, one launch (start us, length us, event | category | flops | bytes accessed | tf_op | source)
XLA Modules:
  0.0 295.4 jit_solution(2438240506324041226)
XLA Ops:
  0.0 0.0 copy-start
  0.0 0.9 copy-done
  1.0 10.3 %fusion.30 = f32[8192,512]{1,0:T(8,128)} fusion(bf16[256,8192]{1,0:T(8,128)(2,1)} %param.2, bf16[256,512]{1,0:T(8,128)(2,1)S(1)} %copy-done), kind=kOutput, calls=%fused_computation.44 | convolution fusion | flops 2147483648 | bytes 21233664 | tf_op jit(solution)/shard_map/dot_general | solution.py:39
  11.2 23.7 %abs_reduce_fusion = (f32[64,512]{1,0:T(8,128)S(1)}, f32[64,512,128]{1,2,0:T(8,128)}) fusion(f32[64,128,512]{2,1,0:T(8,128)} %bitcast.26), kind=kOutput, calls=%fused_computation.3 | convolution fusion | flops 6451396608 | bytes 33685504 | tf_op jit(solution)/shard_map/ij,bjc->bic/dot_general | solution.py:41
  34.9 0.1 fusion.29
  35.0 0.7 reshape.85
  35.6 10.4 %all-to-all-start.1 = ((bf16[16,4,512]{2,1,0:T(4,128)(2,1)}), bf16[16,4,512]{2,1,0:T(4,128)(2,1)S(1)}, u32[]{:S(2)}, u32[]{:S(2)}) async-start(bf16[16,4,512]{2,1,0:T(4,128)(2,1)} %reshape.85), calls=%async_computation.1 | async-start | bytes 131072 | tf_op jit(solution)/shard_map/all_to_all | solution.py:46
  46.1 9.7 %divide_convert_fusion = bf16[64,512,128]{1,2,0:T(8,128)(2,1)} fusion(f32[64,512,128]{1,2,0:T(8,128)} %get-tuple-element.10, f32[64,512]{1,0:T(8,128)S(1)} %get-tuple-element.6), kind=kLoop, calls=%fused_computation.2 | loop fusion | flops 8388608 | bytes 25296896 | tf_op jit(solution)/shard_map/convert_element_type | solution.py:26
  55.8 0.0 all-to-all-done.1
  55.8 7.3 %all-to-all-start = ((bf16[16,512,512]{2,1,0:T(8,128)(2,1)}), bf16[16,512,512]{2,1,0:T(8,128)(2,1)}, u32[]{:S(2)}, u32[]{:S(2)}) async-start(bf16[16,512,512]{2,1,0:T(8,128)(2,1)} %bitcast.27), calls=%async_computation | async-start | bytes 16777216 | tf_op jit(solution)/shard_map/all_to_all | solution.py:43
  63.1 184.2 %all-to-all-done = bf16[16,512,512]{2,1,0:T(8,128)(2,1)} async-done(((bf16[16,512,512]{2,1,0:T(8,128)(2,1)}), bf16[16,512,512]{2,1,0:T(8,128)(2,1)}, u32[]{:S(2)}, u32[]{:S(2)}) %all-to-all-start) | async-done | bytes 8388640 | tf_op jit(solution)/shard_map/all_to_all | solution.py:43
  247.3 5.1 %fusion = f32[512,512]{1,0:T(8,128)S(1)} fusion(bf16[16,512,512]{2,1,0:T(8,128)(2,1)} %all-to-all-done, f32[16,4,512]{2,1,0:T(4,128)S(1)} %convert_element_type.53), kind=kLoop, calls=%fused_computation.1 | loop fusion | flops 12320768 | bytes 9568256 | tf_op jit(solution)/shard_map/reduce_sum | solution.py:54
  252.4 0.1 bitcast_reduce_fusion
  252.6 0.5 broadcast.69
  253.1 0.7 reduce.5
  253.8 0.6 reshape.87
  254.4 10.2 %all-to-all-start.3 = ((bf16[32,2,256]{2,1,0:T(2,128)(2,1)}), bf16[32,2,256]{2,1,0:T(2,128)(2,1)S(1)}, u32[]{:S(2)}, u32[]{:S(2)}) async-start(bf16[32,2,256]{2,1,0:T(2,128)(2,1)} %reshape.87), calls=%async_computation.3 | async-start | bytes 65536 | tf_op jit(solution)/shard_map/all_to_all | solution.py:60
  264.6 0.9 divide_convert_fusion.1
  265.5 7.9 %all-to-all-done.3 = bf16[32,2,256]{2,1,0:T(2,128)(2,1)S(1)} async-done(((bf16[32,2,256]{2,1,0:T(2,128)(2,1)}), bf16[32,2,256]{2,1,0:T(2,128)(2,1)S(1)}, u32[]{:S(2)}, u32[]{:S(2)}) %all-to-all-start.3) | async-done | bytes 32800 | tf_op jit(solution)/shard_map/all_to_all | solution.py:60
  273.4 4.9 %all-to-all-start.2 = ((bf16[32,16,512]{2,1,0:T(8,128)(2,1)}), bf16[32,16,512]{2,1,0:T(8,128)(2,1)S(1)}, u32[]{:S(2)}, u32[]{:S(2)}) async-start(bf16[32,16,512]{2,1,0:T(8,128)(2,1)} %divide_convert_fusion.1), calls=%async_computation.2 | async-start | bytes 1048576 | tf_op jit(solution)/shard_map/all_to_all | solution.py:59
  278.3 16.3 %all-to-all-done.2 = bf16[32,16,512]{2,1,0:T(8,128)(2,1)S(1)} async-done(((bf16[32,16,512]{2,1,0:T(8,128)(2,1)}), bf16[32,16,512]{2,1,0:T(8,128)(2,1)S(1)}, u32[]{:S(2)}, u32[]{:S(2)}) %all-to-all-start.2) | async-done | bytes 524320 | tf_op jit(solution)/shard_map/all_to_all | solution.py:59
  294.7 0.1 multiply_reduce_fusion
  294.8 0.6 broadcast_multiply_fusion
  (6 shorter events, 0.1 us)
Async XLA Ops:
  0.0 1.0 copy-start
  35.6 20.2 %all-to-all-start.1 = ((bf16[16,4,512]{2,1,0:T(4,128)(2,1)}), bf16[16,4,512]{2,1,0:T(4,128)(2,1)S(1)}, u32[]{:S(2)}, u32[]{:S(2)}) async-start(bf16[16,4,512]{2,1,0:T(4,128)(2,1)} %reshape.85), calls=%async_computation.1 | async-start | bytes 131072 | tf_op jit(solution)/shard_map/all_to_all | solution.py:46
  55.8 191.5 %all-to-all-start = ((bf16[16,512,512]{2,1,0:T(8,128)(2,1)}), bf16[16,512,512]{2,1,0:T(8,128)(2,1)}, u32[]{:S(2)}, u32[]{:S(2)}) async-start(bf16[16,512,512]{2,1,0:T(8,128)(2,1)} %bitcast.27), calls=%async_computation | async-start | bytes 16777216 | tf_op jit(solution)/shard_map/all_to_all | solution.py:43
  254.4 19.0 %all-to-all-start.3 = ((bf16[32,2,256]{2,1,0:T(2,128)(2,1)}), bf16[32,2,256]{2,1,0:T(2,128)(2,1)S(1)}, u32[]{:S(2)}, u32[]{:S(2)}) async-start(bf16[32,2,256]{2,1,0:T(2,128)(2,1)} %reshape.87), calls=%async_computation.3 | async-start | bytes 65536 | tf_op jit(solution)/shard_map/all_to_all | solution.py:60
  273.4 21.2 %all-to-all-start.2 = ((bf16[32,16,512]{2,1,0:T(8,128)(2,1)}), bf16[32,16,512]{2,1,0:T(8,128)(2,1)S(1)}, u32[]{:S(2)}, u32[]{:S(2)}) async-start(bf16[32,16,512]{2,1,0:T(8,128)(2,1)} %divide_convert_fusion.1), calls=%async_computation.2 | async-start | bytes 1048576 | tf_op jit(solution)/shard_map/all_to_all | solution.py:59
where the time goes:
time: 296 us; the launch traced here: 295 us
  waiting for transfers between devices  208 us (70%)
  matrix products  34 us (11%)
  starting transfers between devices  32.7 us (11%)
  other arithmetic  17.4 us (6%)
    all_to_all x1, waiting for transfers between devices, per_device(): lax.all_to_all(encoded.reshape(model_width, columns), 'narrow', split_axi...  184 us
    dot_general x1, matrix products, per_device(): jnp.einsum('ij,bjc->bic', rotation, blocked, precision=lax.Precision.HIGH...  23.7 us
    all_to_all x1, waiting for transfers between devices, per_device(): lax.all_to_all(summed, 'wide', split_axis=0, concat_axis=0, tiled=True)  16.3 us
    convert_element_type x2, other arithmetic, encode(): encoded = (values / scales[..., None, :]).astype(jnp.bfloat16)  10.7 us
    all_to_all x1, starting transfers between devices, per_device(): lax.all_to_all(scales, 'narrow', split_axis=0, concat_axis=0, tiled=True)  10.4 us
    dot_general x1, matrix products, per_device(): jnp.dot(activations.T, out_grads, preferred_element_type=jnp.float32)  10.3 us
    all_to_all x1, starting transfers between devices, per_device(): lax.all_to_all(spread, 'wide', split_axis=0, concat_axis=0, tiled=True)  10.2 us
    all_to_all x1, waiting for transfers between devices, per_device(): lax.all_to_all(spread, 'wide', split_axis=0, concat_axis=0, tiled=True)  7.89 us
  transfers between devices with their start and end apart: 4, of which 3 were waited for; matrix products, arithmetic and copies ran while one was open for 4% of the time, Pallas kernels for 0%

commit v1 on v0

v1 whole, which is shorter than its diff:
```python
import functools
import math

import jax
import jax.numpy as jnp
from jax import lax
from jax.experimental import pallas as pl
from jax.experimental.pallas import tpu as pltpu
from jax.sharding import PartitionSpec as P

Z, CORES, X, Y = 8, 2, 4, 8
BLOCK = 128
SUB = 16
TOK = 256
WIDTH = X * BLOCK
COLS = 512
F32, BF16 = jnp.float32, jnp.bfloat16
MESH = pl.DeviceIdType.MESH


def kernel(
    act_ref, grad_ref, out_ref,
    a_buf, g_buf, h_buf, m_buf,
    zs, zr, ys, yr, xs, xr,
    z2s, z2r, y2s, y2r, v2s, v2r, w2s, w2r,
    z3s, z3r, y3s, y3r, v3s, v3r, w3s, w3r,
    z_acc, y_acc, v_acc, w_acc,
    load_sem, gload_sem, asend, arecv, gsend, grecv,
    zssem, zrsem, yssem, yrsem, xssem, xrsem, s2sem, r2sem, s3sem, r3sem,
):
    n = lax.axis_index("narrow")
    w = lax.axis_index("wide")
    z, core = n // CORES, n % CORES
    x, y = w // Y, w % Y
    other = 1 - core

    def at_z(d):
        return (((z + d + Z) % Z) * CORES + core, w)

    def at_y(d):
        return (n, x * Y + (y + d + Y) % Y)

    def at_x(d):
        return (n, ((x + d + X) % X) * Y + y)

    sibling = (z * CORES + other, w)

    def own_load(k):
        return pltpu.make_async_copy(
            act_ref.at[:, pl.ds(k * (CORES * WIDTH) + core * WIDTH, WIDTH)],
            a_buf.at[k, pl.ds(core * TOK, TOK), :],
            load_sem.at[k],
        )

    def swap(k):
        return pltpu.make_async_remote_copy(
            src_ref=act_ref.at[:, pl.ds(k * (CORES * WIDTH) + other * WIDTH, WIDTH)],
            dst_ref=a_buf.at[k, pl.ds(core * TOK, TOK), :],
            send_sem=asend.at[k],
            recv_sem=arecv.at[k],
            device_id=sibling,
            device_id_type=MESH,
        )

    def landed(k):
        return pltpu.make_async_remote_copy(
            src_ref=act_ref.at[:, pl.ds(k * (CORES * WIDTH) + other * WIDTH, WIDTH)],
            dst_ref=a_buf.at[k, pl.ds(other * TOK, TOK), :],
            send_sem=asend.at[k],
            recv_sem=arecv.at[k],
            device_id=sibling,
            device_id_type=MESH,
        )

    def order(i):
        return (z + 4 + i // 2 - (i % 2) * i + 2 * Z) % Z

    g_load = pltpu.make_async_copy(grad_ref, g_buf.at[pl.ds(core * TOK, TOK), :], gload_sem)
    g_swap = pltpu.make_async_remote_copy(
        src_ref=grad_ref,
        dst_ref=g_buf.at[pl.ds(core * TOK, TOK), :],
        send_sem=gsend,
        recv_sem=grecv,
        device_id=sibling,
        device_id_type=MESH,
    )
    g_landed = pltpu.make_async_remote_copy(
        src_ref=grad_ref,
        dst_ref=g_buf.at[pl.ds(other * TOK, TOK), :],
        send_sem=gsend,
        recv_sem=grecv,
        device_id=sibling,
        device_id_type=MESH,
    )
    g_load.start()

    @pl.loop(0, Z)
    def _(i):
        own_load(order(i)).start()

    barrier = pltpu.get_barrier_semaphore()
    pl.semaphore_signal(barrier, inc=1, device_id=sibling, device_id_type=MESH)
    for d in range(1, Z):
        pl.semaphore_signal(barrier, inc=1, device_id=at_z(d), device_id_type=MESH)
    for d in range(1, Y):
        pl.semaphore_signal(barrier, inc=1, device_id=at_y(d), device_id_type=MESH)
    for d in range(1, X):
        pl.semaphore_signal(barrier, inc=1, device_id=at_x(d), device_id_type=MESH)

    row = lax.broadcasted_iota(jnp.int32, (BLOCK, BLOCK), 0)
    col = lax.broadcasted_iota(jnp.int32, (BLOCK, BLOCK), 1)
    bits = row & col
    bits = bits ^ (bits >> 4)
    bits = bits ^ (bits >> 2)
    bits = bits ^ (bits >> 1)
    h_buf[...] = (1 - 2 * (bits & 1)).astype(F32).astype(BF16)

    pl.semaphore_wait(barrier, 1 + (Z - 1) + (Y - 1) + (X - 1))

    g_swap.start()

    @pl.loop(0, Z)
    def _(i):
        swap(order(i)).start()

    g_load.wait()
    g_landed.wait_recv()

    def compute(i):
        k = order(i)
        own_load(k).wait()
        landed(k).wait_recv()
        for b in range(X):
            turned = lax.dot_general(
                h_buf[...],
                a_buf[k, :, b * BLOCK : (b + 1) * BLOCK],
                (((1,), (1,)), ((), ())),
                preferred_element_type=F32,
            ).astype(BF16)
            m_buf[k, b] = jnp.dot(turned, g_buf[...], preferred_element_type=F32)

    def send(src, dst, ssem, rsem, target):
        copy = pltpu.make_async_remote_copy(
            src_ref=src, dst_ref=dst, send_sem=ssem, recv_sem=rsem,
            device_id=target, device_id_type=MESH,
        )
        copy.start()
        return copy

    started = []

    def z_own(d, b):
        return m_buf[d, b, :, 0:128]

    def z_step(k):
        for way in range(2):
            sign = 1 - 2 * way
            dest = (z + sign * (Z // 2 - k) + Z) % Z
            low = 2 * way
            if k == 0:
                for b in range(2):
                    zs[way, 0, b] = z_own(dest, low + b).astype(BF16)
                src, dst = zs.at[way, 0, pl.ds(0, 2)], zr.at[way, 0, pl.ds(0, 2)]
            else:
                started[zi[way, k - 1]].wait_recv()
                for b in range(X):
                    if k == 1:
                        if low <= b < low + 2:
                            zs[way, k, b] = (z_own(dest, b) + zr[way, 0, b - low].astype(F32)).astype(BF16)
                        else:
                            zs[way, k, b] = z_own(dest, b).astype(BF16)
                    else:
                        zs[way, k, b] = (z_own(dest, b) + zr[way, k - 1, b].astype(F32)).astype(BF16)
                src, dst = zs.at[way, k], zr.at[way, k]
            zi[way, k] = len(started)
            started.append(send(src, dst, zssem.at[way, k], zrsem.at[way, k], at_z(sign)))

    def y_own(d, k):
        return m_buf[k, :, pl.ds(pl.multiple_of(d * SUB, SUB), SUB), 128:256]

    def y_step(k):
        for way in range(2):
            sign = 1 - 2 * way
            dest = (y + sign * (Y // 2 - k) + Y) % Y
            low = 4 * way
            if k == 0:
                for p in range(4):
                    ys[way, 0, p] = y_own(dest, low + p).astype(BF16)
                src, dst = ys.at[way, 0, pl.ds(0, 4)], yr.at[way, 0, pl.ds(0, 4)]
            else:
                started[yi[way, k - 1]].wait_recv()
                for p in range(Z):
                    if k == 1:
                        if low <= p < low + 4:
                            ys[way, k, p] = (y_own(dest, p) + yr[way, 0, p - low].astype(F32)).astype(BF16)
                        else:
                            ys[way, k, p] = y_own(dest, p).astype(BF16)
                    else:
                        ys[way, k, p] = (y_own(dest, p) + yr[way, k - 1, p].astype(F32)).astype(BF16)
                src, dst = ys.at[way, k], yr.at[way, k]
            yi[way, k] = len(started)
            started.append(send(src, dst, yssem.at[way, k], yrsem.at[way, k], at_y(sign)))

    def x_own(d, k):
        return m_buf[k, d, :, 256:512]

    def x_step(k):
        for way in range(2):
            sign = 1 - 2 * way
            dest = (x + sign * (X // 2 - k) + X) % X
            low = 4 * way
            if k == 0:
                @pl.loop(0, 4)
                def _(p):
                    xs[way, 0, p] = x_own(dest, low + p).astype(BF16)
                src, dst = xs.at[way, 0, pl.ds(0, 4)], xr.at[way, 0, pl.ds(0, 4)]
            else:
                started[xi[way, k - 1]].wait_recv()

                @pl.loop(0, 4)
                def _(p):
                    xs[way, 1, low + p] = (x_own(dest, low + p) + xr[way, 0, p].astype(F32)).astype(BF16)
                    xs[way, 1, 4 - low + p] = x_own(dest, 4 - low + p).astype(BF16)
                src, dst = xs.at[way, k], xr.at[way, k]
            xi[way, k] = len(started)
            started.append(send(src, dst, xssem.at[way, k], xrsem.at[way, k], at_x(sign)))

    zi, yi, xi = {}, {}, {}

    compute(0)
    z_step(0)

    @pl.loop(1, Z)
    def _(i):
        compute(i)

    x_step(0)
    y_step(0)
    z_step(1)
    y_step(1)
    z_step(2)
    y_step(2)
    x_step(1)
    z_step(3)
    y_step(3)

    def drain(buf, sem):
        pltpu.make_async_copy(buf, buf, sem).wait()

    def rows_of(d):
        return pl.ds(pl.multiple_of(d * SUB, SUB), SUB)

    for way in range(2):
        started[zi[way, 3]].wait_recv()
    for j in range(1, Y + 1):
        d = (y + j) % Y
        part = (
            m_buf[z, :, rows_of(d), 0:128]
            + zr[0, 3, :, rows_of(d), :].astype(F32)
            + zr[1, 3, :, rows_of(d), :].astype(F32)
        )
        if j < Y:
            z2s[j - 1] = part.astype(BF16)
            send(z2s.at[j - 1], z2r.at[j - 1], s2sem.at[0], r2sem.at[0], at_y(j))
        else:
            z_acc[...] = part

    for way in range(2):
        started[yi[way, 3]].wait_recv()
    for j in range(1, Z + 1):
        d = (z + j) % Z
        part = (
            m_buf[d, :, rows_of(y), 128:256]
            + yr[0, 3, d].astype(F32)
            + yr[1, 3, d].astype(F32)
        )
        if j < Z:
            y2s[j - 1] = part.astype(BF16)
            send(y2s.at[j - 1], y2r.at[j - 1], s2sem.at[1], r2sem.at[1], at_z(j))
        else:
            y_acc[...] = part

    def x_third(s2, r2, acc, s3, r3, at):
        drain(r2, r2sem.at[at])
        for j in range(1, X + 1):
            d = (x + j) % X
            part = acc[d]
            for q in range(r2.shape[0]):
                part = part + r2[q, d].astype(F32)
            if j < X:
                s3[j - 1] = part.astype(BF16)
                send(s3.at[j - 1], r3.at[j - 1], s3sem.at[at], r3sem.at[at], at_x(j))
            else:
                acc[0] = part

    x_third(z2s, z2r, z_acc, z3s, z3r, 0)
    x_third(y2s, y2r, y_acc, y3s, y3r, 1)

    for way in range(2):
        started[xi[way, 1]].wait_recv()
    for j in range(1, Y + 1):
        d = (y + j) % Y
        part = (
            m_buf[:, x, rows_of(d), 256:384]
            + xr[0, 1, :, rows_of(d), 0:128].astype(F32)
            + xr[1, 1, :, rows_of(d), 0:128].astype(F32)
        )
        if j < Y:
            v2s[j - 1] = part.astype(BF16)
            send(v2s.at[j - 1], v2r.at[j - 1], s2sem.at[2], r2sem.at[2], at_y(j))
        else:
            v_acc[...] = part
        d = (z + j) % Z
        part = (
            m_buf[d, x, :, 384:512]
            + xr[0, 1, d, :, 128:256].astype(F32)
            + xr[1, 1, d, :, 128:256].astype(F32)
        )
        if j < Z:
            w2s[j - 1] = part.astype(BF16)
            send(w2s.at[j - 1], w2r.at[j - 1], s2sem.at[3], r2sem.at[3], at_z(j))
        else:
            w_acc[...] = part

    scale = 1.0 / (Z * CORES * X * Y * math.sqrt(BLOCK))

    def finish(own, r3, at, first):
        drain(r3, r3sem.at[at])
        total = own
        for q in range(r3.shape[0]):
            total = total + r3[q].astype(F32)
        out_ref[:, first : first + 128] = total * scale

    finish(z_acc[0], z3r, 0, 0)
    finish(y_acc[0], y3r, 1, 128)

    drain(v2r, r2sem.at[2])
    for j in range(1, Z + 1):
        d = (z + j) % Z
        part = v_acc[d]
        for q in range(Y - 1):
            part = part + v2r[q, d].astype(F32)
        if j < Z:
            v3s[j - 1] = part.astype(BF16)
            send(v3s.at[j - 1], v3r.at[j - 1], s3sem.at[2], r3sem.at[2], at_z(j))
        else:
            v_own = part
    drain(w2r, r2sem.at[3])
    for j in range(1, Y + 1):
        d = (y + j) % Y
        part = w_acc[rows_of(d), :]
        for q in range(Z - 1):
            part = part + w2r[q, rows_of(d), :].astype(F32)
        if j < Y:
            w3s[j - 1] = part.astype(BF16)
            send(w3s.at[j - 1], w3r.at[j - 1], s3sem.at[3], r3sem.at[3], at_y(j))
        else:
            w_own = part
    finish(v_own, v3r, 2, 256)
    finish(w_own, w3r, 3, 384)

    g_swap.wait_send()

    @pl.loop(0, Z)
    def _(k):
        swap(k).wait_send()

    for copy in started:
        copy.wait_send()
    for at, buf in enumerate((z2s, y2s, v2s, w2s)):
        drain(buf, s2sem.at[at])
    for at, buf in enumerate((z3s, y3s, v3s, w3s)):
        drain(buf, s3sem.at[at])


def per_device(activations, out_grads):
    def vm(*shape, dtype=BF16):
        return pltpu.VMEM(shape, dtype)

    dma = pltpu.SemaphoreType.DMA
    scratch = [
        vm(Z, CORES * TOK, WIDTH), vm(CORES * TOK, COLS), vm(BLOCK, BLOCK),
        vm(Z, X, BLOCK, COLS, dtype=F32),
        vm(2, 4, X, BLOCK, 128), vm(2, 4, X, BLOCK, 128),
        vm(2, 4, Z, X, SUB, 128), vm(2, 4, Z, X, SUB, 128),
        vm(2, 2, Z, BLOCK, 256), vm(2, 2, Z, BLOCK, 256),
        vm(Y - 1, X, SUB, 128), vm(Y - 1, X, SUB, 128),
        vm(Z - 1, X, SUB, 128), vm(Z - 1, X, SUB, 128),
        vm(Y - 1, Z, SUB, 128), vm(Y - 1, Z, SUB, 128),
        vm(Z - 1, BLOCK, 128), vm(Z - 1, BLOCK, 128),
        vm(X - 1, SUB, 128), vm(X - 1, SUB, 128),
        vm(X - 1, SUB, 128), vm(X - 1, SUB, 128),
        vm(Z - 1, SUB, 128), vm(Z - 1, SUB, 128),
        vm(Y - 1, SUB, 128), vm(Y - 1, SUB, 128),
        vm(X, SUB, 128, dtype=F32), vm(X, SUB, 128, dtype=F32),
        vm(Z, SUB, 128, dtype=F32), vm(BLOCK, 128, dtype=F32),
        dma((Z,)), dma, dma((Z,)), dma((Z,)), dma, dma,
        dma((2, 4)), dma((2, 4)), dma((2, 4)), dma((2, 4)), dma((2, 2)), dma((2, 2)),
        dma((4,)), dma((4,)), dma((4,)), dma((4,)),
    ]
    return pl.pallas_call(
        kernel,
        out_shape=jax.ShapeDtypeStruct((SUB, COLS), F32),
        in_specs=[pl.BlockSpec(memory_space=pl.ANY)] * 2,
        out_specs=pl.BlockSpec(memory_space=pltpu.VMEM),
        scratch_shapes=scratch,
        compiler_params=pltpu.CompilerParams(
            collective_id=0, has_side_effects=True, vmem_limit_bytes=48 * 1024 * 1024
        ),
        cost_estimate=pl.CostEstimate(
            flops=2 * CORES * TOK * Z * WIDTH * (COLS + BLOCK),
            bytes_accessed=TOK * (2 * Z * WIDTH + COLS) * 2,
            transcendentals=0,
        ),
    )(activations, out_grads)


def solution(mesh):
    return jax.shard_map(
        per_device,
        mesh=mesh,
        in_specs=(P(("narrow", "wide"), None), P(("narrow", "wide"), None)),
        out_specs=P(("narrow", "wide"), None),
        check_vma=False,
    )
```

time: 296 us -> 64.9 us (0.22)
  the two profiles are of different devices: /device:TPU:8 before, /device:TPU:6 now
where the time goes in v1:
time: 64.9 us; the launch traced here: 64.7 us
  Pallas kernels  60.9 us (94%)
  local copies, waits for them, and re-layouts  3.75 us (6%)
    pallas_call x1, Pallas kernels, per_device(): pl.pallas_call(kernel, out_shape=jax.ShapeDtypeStruct((SUB, COLS), F32),...  60.9 us
    unnamed x5, local copies, waits for them, and re-layouts  3.75 us

profile of v1, /device:TPU:6, one launch (start us, length us, event | category | flops | bytes accessed | tf_op | source)
XLA Modules:
  0.0 64.7 jit_solution(3021583189130543655)
XLA Ops:
  0.0 0.0 copy-start
  0.0 2.2 %copy-done = bf16[256,8192]{1,0:T(8,128)(2,1)S(1)} copy-done((bf16[256,8192]{1,0:T(8,128)(2,1)S(1)}, bf16[256,8192]{1,0:T(8,128)(2,1)}, u32[]{:S(2)}) %copy-start) | copy-done | bytes 4194328
  2.2 0.0 copy-start.1
  2.2 0.9 %copy-done.1 = bf16[256,512]{1,0:T(8,128)(2,1)S(1)} copy-done((bf16[256,512]{1,0:T(8,128)(2,1)S(1)}, bf16[256,512]{1,0:T(8,128)(2,1)}, u32[]{:S(2)}) %copy-start.1) | copy-done | bytes 262168
  3.1 60.9 %shard_map.28 = f32[16,512]{1,0:T(8,128)S(1)} custom-call(bf16[256,8192]{1,0:T(8,128)(2,1)S(1)} %copy-done, bf16[256,512]{1,0:T(8,128)(2,1)S(1)} %copy-done.1), custom_call_target="tpu_custom_call" | custom-call | flops 2684354560 | bytes 4456448 | tf_op jit(solution)/shard_map/pallas_call | solution.py:401
  64.1 0.6 copy.4
Async XLA Ops:
  0.0 2.2 %copy-start = (bf16[256,8192]{1,0:T(8,128)(2,1)S(1)}, bf16[256,8192]{1,0:T(8,128)(2,1)}, u32[]{:S(2)}) copy-start(bf16[256,8192]{1,0:T(8,128)(2,1)} %act_ref.1) | copy-start | bytes 12582916
  2.2 0.9 %copy-start.1 = (bf16[256,512]{1,0:T(8,128)(2,1)S(1)}, bf16[256,512]{1,0:T(8,128)(2,1)}, u32[]{:S(2)}) copy-start(bf16[256,512]{1,0:T(8,128)(2,1)} %grad_ref.1) | copy-start | bytes 786436

commit v2 on v0

v2 whole, which is shorter than its diff:
```python
import math

import jax
import jax.numpy as jnp
from jax import lax
from jax.experimental import pallas as pl
from jax.experimental.pallas import tpu as pltpu
from jax.sharding import PartitionSpec as P

Z, CORES, X, Y = 8, 2, 4, 8
BLOCK = 128
HALF = BLOCK // 2
SUB = 16
TOK = 256
WIDTH = X * BLOCK
COLS = 512
F32, BF16 = jnp.float32, jnp.bfloat16
MESH = pl.DeviceIdType.MESH

OFFSET = (4, 3, 5, 2, 6, 1, 7, 0)
STEP = {offset: i for i, offset in enumerate(OFFSET)}


def kernel(
    act_ref, grad_ref, out_ref,
    a_buf, g_buf, h_buf, m_buf,
    zs, zr, ys, yr, xs0, xr0, xs1, xr1, vs, vr,
    z2s, z2r, y2s, y2r, v2s, v2r, z3s, z3r, y3s, y3r,
    z_acc, y_acc,
    load_sem, gload_sem, asend, arecv, gsend, grecv,
    zssem, zrsem, yssem, yrsem, x0ssem, x0rsem, x1ssem, x1rsem, vssem, vrsem,
    s2sem, r2sem, s3sem, r3sem,
):
    n = lax.axis_index("narrow")
    w = lax.axis_index("wide")
    z, core = n // CORES, n % CORES
    x, y = w // Y, w % Y
    other = 1 - core

    def at_z(d):
        return (((z + d + Z) % Z) * CORES + core, w)

    def at_y(d):
        return (n, x * Y + (y + d + Y) % Y)

    def at_x(d):
        return (n, ((x + d + X) % X) * Y + y)

    sibling = (z * CORES + other, w)

    def remote(src, dst, ssem, rsem, target):
        return pltpu.make_async_remote_copy(
            src_ref=src, dst_ref=dst, send_sem=ssem, recv_sem=rsem,
            device_id=target, device_id_type=MESH,
        )

    def place(i):
        return (z + 4 + i // 2 - (i % 2) * i + 2 * Z) % Z

    def own_load(i):
        return pltpu.make_async_copy(
            act_ref.at[:, pl.ds((place(i) * CORES + core) * WIDTH, WIDTH)],
            a_buf.at[i, pl.ds(core * TOK, TOK), :],
            load_sem.at[i],
        )

    def swap(i, half):
        return remote(
            act_ref.at[:, pl.ds((place(i) * CORES + other) * WIDTH, WIDTH)],
            a_buf.at[i, pl.ds(half * TOK, TOK), :],
            asend.at[i], arecv.at[i], sibling,
        )

    def g_swap(half):
        return remote(grad_ref, g_buf.at[pl.ds(half * TOK, TOK), :], gsend, grecv, sibling)

    g_load = pltpu.make_async_copy(grad_ref, g_buf.at[pl.ds(core * TOK, TOK), :], gload_sem)

    barrier = pltpu.get_barrier_semaphore()
    pl.semaphore_signal(barrier, inc=1, device_id=sibling, device_id_type=MESH)
    for d in range(1, Z):
        pl.semaphore_signal(barrier, inc=1, device_id=at_z(d), device_id_type=MESH)
    for d in range(1, Y):
        pl.semaphore_signal(barrier, inc=1, device_id=at_y(d), device_id_type=MESH)
    for d in range(1, X):
        pl.semaphore_signal(barrier, inc=1, device_id=at_x(d), device_id_type=MESH)

    g_load.start()

    @pl.loop(0, Z)
    def _(i):
        own_load(i).start()

    row = (lax.broadcasted_iota(jnp.int32, (BLOCK, BLOCK), 0) + y * SUB) & (BLOCK - 1)
    col = lax.broadcasted_iota(jnp.int32, (BLOCK, BLOCK), 1)
    bits = row & col
    bits = bits ^ (bits >> 4)
    bits = bits ^ (bits >> 2)
    bits = bits ^ (bits >> 1)
    h_buf[...] = (1 - 2 * (bits & 1)).astype(F32).astype(BF16)

    pl.semaphore_wait(barrier, 1 + (Z - 1) + (Y - 1) + (X - 1))

    g_swap(core).start()

    @pl.loop(0, Z)
    def _(i):
        swap(i, core).start()

    def compute(i):
        own_load(i).wait()
        swap(i, other).wait_recv()
        for j in range(X):
            b = (x + j) % X
            turned = lax.dot_general(
                h_buf[...],
                a_buf[i, :, pl.ds(pl.multiple_of(b * BLOCK, BLOCK), BLOCK)],
                (((1,), (1,)), ((), ())),
                preferred_element_type=F32,
            ).astype(BF16)
            m_buf[i, j] = jnp.dot(turned, g_buf[...], preferred_element_type=F32)

    def way_sign(way):
        return 1 - 2 * way

    def z_copy(way, h, k):
        return remote(
            zs.at[way, h, k], zr.at[way, h, k], zssem.at[way, h, k], zrsem.at[way, h, k],
            at_z(way_sign(way)),
        )

    def z_step(way, h, k):
        i = STEP[(way_sign(way) * (4 - k)) % Z]
        if k >= 2 or (k == 1 and h == way):
            z_copy(way, h, k - 1).wait_recv()
            for j in range(2):
                zs[way, h, k, j] = (
                    m_buf[i, 2 * h + j, :, 0:128] + zr[way, h, k - 1, j].astype(F32)
                ).astype(BF16)
        else:
            for j in range(2):
                zs[way, h, k, j] = m_buf[i, 2 * h + j, :, 0:128].astype(BF16)
        z_copy(way, h, k).start()

    def y_copy(way, g, k):
        return remote(
            ys.at[way, g, k], yr.at[way, g, k], yssem.at[way, g, k], yrsem.at[way, g, k],
            at_y(way_sign(way)),
        )

    def y_step(way, g, k):
        first = ((way_sign(way) * (4 - k)) % Y) * SUB
        if k >= 2 or (k == 1 and g == way):
            y_copy(way, g, k - 1).wait_recv()
            for p in range(4):
                ys[way, g, k, p] = (
                    m_buf[4 * g + p, :, first : first + SUB, 128:256]
                    + yr[way, g, k - 1, p].astype(F32)
                ).astype(BF16)
        else:
            for p in range(4):
                ys[way, g, k, p] = m_buf[4 * g + p, :, first : first + SUB, 128:256].astype(BF16)
        y_copy(way, g, k).start()

    def x0_copy(way, i):
        return remote(
            xs0.at[i, way], xr0.at[i, way], x0ssem.at[i, way], x0rsem.at[i, way],
            at_x(way_sign(way)),
        )

    def x1_copy(way, i):
        return remote(
            xs1.at[i, way], xr1.at[i, way], x1ssem.at[i, way], x1rsem.at[i, way],
            at_x(way_sign(way)),
        )

    def v_copy(way, k):
        if k == 0:
            src, dst = vs.at[way, 0, pl.ds(0, HALF)], vr.at[way, 0, pl.ds(0, HALF)]
        else:
            src, dst = vs.at[way, k], vr.at[way, k]
        return remote(src, dst, vssem.at[way, k], vrsem.at[way, k], at_z(way_sign(way)))

    def x0_step(i):
        for way in range(2):
            xs0[i, way] = m_buf[i, 2, way * HALF : (way + 1) * HALF, 256:512].astype(BF16)
            x0_copy(way, i).start()

    def x1_step(i):
        for way in range(2):
            j = 1 + 2 * way
            x0_copy(way, i).wait_recv()
            mine = slice(way * HALF, (way + 1) * HALF)
            rest = slice((1 - way) * HALF, (2 - way) * HALF)
            xs1[i, way, mine] = (m_buf[i, j, mine, 256:512] + xr0[i, way].astype(F32)).astype(BF16)
            xs1[i, way, rest] = m_buf[i, j, rest, 256:512].astype(BF16)
            x1_copy(way, i).start()

    def x2_rows(i, rows):
        return (
            m_buf[i, 0, rows, 256:512]
            + xr1[i, 0, rows].astype(F32)
            + xr1[i, 1, rows].astype(F32)
        )

    def x2_step(i):
        for way in range(2):
            x1_copy(way, i).wait_recv()
        if i == 0:
            for way in range(2):
                vs[way, 0, 0:HALF] = x2_rows(0, slice(way * HALF, (way + 1) * HALF)).astype(BF16)
                v_copy(way, 0).start()
        elif i < Z - 1:
            way, k = 1 - i % 2, (i + 1) // 2
            v_copy(way, k - 1).wait_recv()
            if k == 1:
                mine = slice(way * HALF, (way + 1) * HALF)
                rest = slice((1 - way) * HALF, (2 - way) * HALF)
                vs[way, 1, mine] = (x2_rows(i, mine) + vr[way, 0, 0:HALF].astype(F32)).astype(BF16)
                vs[way, 1, rest] = x2_rows(i, rest).astype(BF16)
            else:
                vs[way, k] = (x2_rows(i, slice(0, BLOCK)) + vr[way, k - 1].astype(F32)).astype(BF16)
            v_copy(way, k).start()
        else:
            for way in range(2):
                v_copy(way, 3).wait_recv()
            own = None
            for j in range(Y):
                rows = slice(j * SUB, (j + 1) * SUB)
                part = x2_rows(i, rows) + vr[0, 3, rows].astype(F32) + vr[1, 3, rows].astype(F32)
                if j == 0:
                    own = part
                else:
                    v2s[j - 1] = part.astype(BF16)
                    remote(v2s.at[j - 1], v2r.at[j - 1], s2sem.at[2], r2sem.at[2], at_y(j)).start()
            return own

    def drain(buf, sem):
        pltpu.make_async_copy(buf, buf, sem).wait()

    def z_second():
        for way in range(2):
            for h in range(2):
                z_copy(way, h, 3).wait_recv()
        for j in range(Y):
            rows = slice(j * SUB, (j + 1) * SUB)
            for h in range(2):
                part = (
                    m_buf[Z - 1, 2 * h : 2 * h + 2, rows, 0:128]
                    + zr[0, h, 3, :, rows].astype(F32)
                    + zr[1, h, 3, :, rows].astype(F32)
                )
                if j == 0:
                    z_acc[2 * h : 2 * h + 2] = part
                else:
                    z2s[j - 1, 2 * h : 2 * h + 2] = part.astype(BF16)
            if j > 0:
                remote(z2s.at[j - 1], z2r.at[j - 1], s2sem.at[0], r2sem.at[0], at_y(j)).start()

    def y_second():
        for way in range(2):
            for g in range(2):
                y_copy(way, g, 3).wait_recv()
        for j in range(Z):
            i = STEP[j]
            part = (
                m_buf[i, :, 0:SUB, 128:256]
                + yr[0, i // 4, 3, i % 4].astype(F32)
                + yr[1, i // 4, 3, i % 4].astype(F32)
            )
            if j == 0:
                y_acc[...] = part
            else:
                y2s[j - 1] = part.astype(BF16)
                remote(y2s.at[j - 1], y2r.at[j - 1], s2sem.at[1], r2sem.at[1], at_z(j)).start()

    def third(r2, acc, s3, r3, at):
        drain(r2, r2sem.at[at])
        own = None
        for j in range(X):
            part = acc[j]
            for q in range(r2.shape[0]):
                part = part + r2[q, j].astype(F32)
            if j == 0:
                own = part
            else:
                s3[j - 1] = part.astype(BF16)
                remote(s3.at[j - 1], r3.at[j - 1], s3sem.at[at], r3sem.at[at], at_x(j)).start()
        return own

    scale = 1.0 / (Z * CORES * X * Y * math.sqrt(BLOCK))

    def finish(own, received, sem, first, last):
        drain(received, sem)
        total = own
        for q in range(received.shape[0]):
            total = total + received[q].astype(F32)
        out_ref[:, first:last] = total * scale

    g_load.wait()
    g_swap(other).wait_recv()

    @pl.loop(0, Z)
    def _(i):
        compute(i)
        x0_step(i)

        @pl.when(i == 0)
        def _():
            z_step(0, 0, 0)
            z_step(1, 1, 0)

        @pl.when(i == 2)
        def _():
            z_step(0, 1, 1)
            z_step(1, 0, 1)

        @pl.when(i == 3)
        def _():
            y_step(0, 0, 0)
            y_step(1, 0, 1)

    y_step(1, 1, 0)
    y_step(0, 1, 1)
    z_step(0, 0, 1)
    z_step(1, 1, 1)
    x1_step(0)
    y_step(0, 0, 1)
    y_step(1, 0, 2)
    x1_step(1)
    z_step(0, 1, 2)
    z_step(1, 0, 2)
    x1_step(2)
    y_step(1, 1, 1)
    y_step(0, 1, 2)
    x2_step(0)
    x1_step(3)
    z_step(0, 0, 2)
    z_step(1, 1, 2)
    x2_step(1)
    y_step(0, 0, 2)
    y_step(1, 0, 3)
    x1_step(4)
    z_step(0, 1, 3)
    z_step(1, 0, 3)
    x2_step(2)
    x1_step(5)
    y_step(1, 1, 2)
    y_step(0, 1, 3)
    z_step(0, 0, 3)
    z_step(1, 1, 3)
    x2_step(3)
    x1_step(6)
    y_step(0, 0, 3)
    y_step(1, 1, 3)
    x1_step(7)
    x2_step(4)
    z_second()
    x2_step(5)
    y_second()
    x2_step(6)
    z_own = third(z2r, z_acc, z3s, z3r, 0)
    y_own = third(y2r, y_acc, y3s, y3r, 1)
    v_own = x2_step(7)
    finish(z_own, z3r, r3sem.at[0], 0, 128)
    finish(y_own, y3r, r3sem.at[1], 128, 256)
    finish(v_own, v2r, r2sem.at[2], 256, 512)

    g_swap(core).wait_send()

    @pl.loop(0, Z)
    def _(i):
        swap(i, core).wait_send()
        for way in range(2):
            x0_copy(way, i).wait_send()
            x1_copy(way, i).wait_send()

    for way in range(2):
        for k in range(4):
            v_copy(way, k).wait_send()
            for part in range(2):
                if k > 0 or part == way:
                    z_copy(way, part, k).wait_send()
                    y_copy(way, part, k).wait_send()
    for at, buf in enumerate((z2s, y2s, v2s)):
        drain(buf, s2sem.at[at])
    for at, buf in enumerate((z3s, y3s)):
        drain(buf, s3sem.at[at])


def per_device(activations, out_grads):
    def vm(*shape, dtype=BF16):
        return pltpu.VMEM(shape, dtype)

    dma = pltpu.SemaphoreType.DMA
    scratch = [
        vm(Z, CORES * TOK, WIDTH), vm(CORES * TOK, COLS), vm(BLOCK, BLOCK),
        vm(Z, X, BLOCK, COLS, dtype=F32),
        vm(2, 2, 4, 2, BLOCK, 128), vm(2, 2, 4, 2, BLOCK, 128),
        vm(2, 2, 4, 4, X, SUB, 128), vm(2, 2, 4, 4, X, SUB, 128),
        vm(Z, 2, HALF, 256), vm(Z, 2, HALF, 256),
        vm(Z, 2, BLOCK, 256), vm(Z, 2, BLOCK, 256),
        vm(2, 4, BLOCK, 256), vm(2, 4, BLOCK, 256),
        vm(Y - 1, X, SUB, 128), vm(Y - 1, X, SUB, 128),
        vm(Z - 1, X, SUB, 128), vm(Z - 1, X, SUB, 128),
        vm(Y - 1, SUB, 256), vm(Y - 1, SUB, 256),
        vm(X - 1, SUB, 128), vm(X - 1, SUB, 128),
        vm(X - 1, SUB, 128), vm(X - 1, SUB, 128),
        vm(X, SUB, 128, dtype=F32), vm(X, SUB, 128, dtype=F32),
        dma((Z,)), dma, dma((Z,)), dma((Z,)), dma, dma,
        dma((2, 2, 4)), dma((2, 2, 4)), dma((2, 2, 4)), dma((2, 2, 4)),
        dma((Z, 2)), dma((Z, 2)), dma((Z, 2)), dma((Z, 2)), dma((2, 4)), dma((2, 4)),
        dma((3,)), dma((3,)), dma((2,)), dma((2,)),
    ]
    return pl.pallas_call(
        kernel,
        out_shape=jax.ShapeDtypeStruct((SUB, COLS), F32),
        in_specs=[pl.BlockSpec(memory_space=pl.ANY)] * 2,
        out_specs=pl.BlockSpec(memory_space=pltpu.VMEM),
        scratch_shapes=scratch,
        compiler_params=pltpu.CompilerParams(
            collective_id=0, has_side_effects=True, vmem_limit_bytes=60 * 1024 * 1024
        ),
        cost_estimate=pl.CostEstimate(
            flops=2 * CORES * TOK * Z * WIDTH * (COLS + BLOCK),
            bytes_accessed=TOK * (2 * Z * WIDTH + COLS) * 2,
            transcendentals=0,
        ),
    )(activations, out_grads)


def solution(mesh):
    return jax.shard_map(
        per_device,
        mesh=mesh,
        in_specs=(P(("narrow", "wide"), None), P(("narrow", "wide"), None)),
        out_specs=P(("narrow", "wide"), None),
        check_vma=False,
    )
```

time: 296 us -> 55.8 us (0.19)
  waiting for transfers between devices: 208 us -> 0 us
  Pallas kernels: 0 us -> 54.2 us
  matrix products: 34 us -> 0 us
  starting transfers between devices: 32.7 us -> 0 us
  other arithmetic: 17.4 us -> 0 us
    all_to_all x4 -> x0, waiting for transfers between devices: 208 us -> none  [the longest x1 184 us: per_device(): lax.all_to_all(encoded.reshape(model_width, columns), 'narrow', split_axi...]
    pallas_call x0 -> x1, Pallas kernels: none -> 54.2 us  [per_device(): pl.pallas_call(kernel, out_shape=jax.ShapeDtypeStruct((SUB, COLS), F32),...]
    dot_general x2 -> x0, matrix products: 34 us -> none  [the longest x1 23.7 us: per_device(): jnp.einsum('ij,bjc->bic', rotation, blocked, precision=lax.Precision.HIGH...]
    all_to_all x4 -> x0, starting transfers between devices: 32.7 us -> none  [the longest x1 10.4 us: per_device(): lax.all_to_all(scales, 'narrow', split_axis=0, concat_axis=0, tiled=True)]
    convert_element_type x5 -> x0, other arithmetic: 10.7 us -> none  [the longest x2 10.7 us: encode(): encoded = (values / scales[..., None, :]).astype(jnp.bfloat16)]
    reduce_sum x2 -> x0, other arithmetic: 5.27 us -> none  [the longest x1 5.13 us: per_device(): summed, summed_scales = encode(jnp.sum(dequantized, axis=0))]
  transfers between devices with their start and end apart: 4 -> 0, of which waited for: 3 -> 0; matrix products, arithmetic and copies ran while one was open for 4% -> 0% of each run, Pallas kernels for 0% -> 0%
where the time goes in v2:
time: 55.8 us; the launch traced here: 55.6 us
  Pallas kernels  54.2 us (97%)
  local copies, waits for them, and re-layouts  1.38 us (2%)
    pallas_call x1, Pallas kernels, per_device(): pl.pallas_call(kernel, out_shape=jax.ShapeDtypeStruct((SUB, COLS), F32),...  54.2 us
    unnamed x1, local copies, waits for them, and re-layouts  1.38 us

profile of v2, /device:TPU:8, one launch (start us, length us, event | category | flops | bytes accessed | tf_op | source)
XLA Modules:
  0.0 55.6 jit_solution(11724914653821404772)
XLA Ops:
  0.0 54.2 %shard_map.28 = f32[16,512]{1,0:T(8,128)} custom-call(bf16[256,8192]{1,0:T(8,128)(2,1)} %act_ref.1, bf16[256,512]{1,0:T(8,128)(2,1)} %grad_ref.1), custom_call_target="tpu_custom_call" | custom-call | flops 2684354560 | bytes 4456448 | tf_op jit(solution)/shard_map/pallas_call | solution.py:415
  54.2 1.4 %copy.4 = f32[16,512]{1,0:T(8,128)} copy(f32[16,512]{1,0:T(8,128)} %shard_map.28) | data formatting | bytes 65536

commit v3 on v2

v3 whole, which is shorter than its diff:
```python
import math

import jax
import jax.numpy as jnp
from jax import lax
from jax.experimental import pallas as pl
from jax.experimental.pallas import tpu as pltpu
from jax.sharding import PartitionSpec as P

Z, CORES, X, Y = 8, 2, 4, 8
BLOCK = 128
HALF = BLOCK // 2
SUB = 16
TOK = 256
WIDTH = X * BLOCK
COLS = 512
F32, BF16 = jnp.float32, jnp.bfloat16
MESH = pl.DeviceIdType.MESH

OFFSET = (4, 3, 5, 2, 6, 1, 7, 0)
STEP = {offset: i for i, offset in enumerate(OFFSET)}
AHEAD = 3


def kernel(
    act_ref, grad_ref, out_ref,
    a_buf, g_buf, h_buf, t_buf, m_buf,
    zs, zr, ys, yr, xs0, xr0, xs1, xr1, vs, vr,
    z2s, z2r, y2s, y2r, v2s, v2r, z3s, z3r, y3s, y3r,
    z_acc, y_acc, v_acc,
    load_sem, gload_sem, asend, arecv, gsend, grecv,
    zssem, zrsem, yssem, yrsem, x0ssem, x0rsem, x1ssem, x1rsem, vssem, vrsem,
    s2sem, r2sem, s3sem, r3sem,
):
    n = lax.axis_index("narrow")
    w = lax.axis_index("wide")
    z, core = n // CORES, n % CORES
    x, y = w // Y, w % Y
    other = 1 - core

    def at_z(d):
        return (((z + d + Z) % Z) * CORES + core, w)

    def at_y(d):
        return (n, x * Y + (y + d + Y) % Y)

    def at_x(d):
        return (n, ((x + d + X) % X) * Y + y)

    sibling = (z * CORES + other, w)

    def remote(src, dst, ssem, rsem, target):
        return pltpu.make_async_remote_copy(
            src_ref=src, dst_ref=dst, send_sem=ssem, recv_sem=rsem,
            device_id=target, device_id_type=MESH,
        )

    def place(i):
        return (z + 4 + i // 2 - (i % 2) * i + 2 * Z) % Z

    def own_load(i):
        return pltpu.make_async_copy(
            act_ref.at[:, pl.ds((place(i) * CORES + core) * WIDTH, WIDTH)],
            a_buf.at[i, pl.ds(core * TOK, TOK), :],
            load_sem.at[i],
        )

    def swap(i, half):
        return remote(
            act_ref.at[:, pl.ds((place(i) * CORES + other) * WIDTH, WIDTH)],
            a_buf.at[i, pl.ds(half * TOK, TOK), :],
            asend.at[i], arecv.at[i], sibling,
        )

    def g_swap(half):
        return remote(grad_ref, g_buf.at[pl.ds(half * TOK, TOK), :], gsend, grecv, sibling)

    g_load = pltpu.make_async_copy(grad_ref, g_buf.at[pl.ds(core * TOK, TOK), :], gload_sem)

    barrier = pltpu.get_barrier_semaphore()
    pl.semaphore_signal(barrier, inc=1, device_id=sibling, device_id_type=MESH)
    for d in range(1, Z):
        pl.semaphore_signal(barrier, inc=1, device_id=at_z(d), device_id_type=MESH)
    for d in range(1, Y):
        pl.semaphore_signal(barrier, inc=1, device_id=at_y(d), device_id_type=MESH)
    for d in range(1, X):
        pl.semaphore_signal(barrier, inc=1, device_id=at_x(d), device_id_type=MESH)

    g_load.start()

    @pl.loop(0, Z)
    def _(i):
        own_load(i).start()

    row = (lax.broadcasted_iota(jnp.int32, (BLOCK, BLOCK), 0) + y * SUB) & (BLOCK - 1)
    col = lax.broadcasted_iota(jnp.int32, (BLOCK, BLOCK), 1)
    bits = row & col
    bits = bits ^ (bits >> 4)
    bits = bits ^ (bits >> 2)
    bits = bits ^ (bits >> 1)
    h_buf[...] = (1 - 2 * (bits & 1)).astype(F32).astype(BF16)

    pl.semaphore_wait(barrier, 1 + (Z - 1) + (Y - 1) + (X - 1))

    g_swap(core).start()

    for i in range(AHEAD):
        swap(i, core).start()

    def compute(i):
        own_load(i).wait()
        swap(i, other).wait_recv()
        if i + AHEAD < Z:
            swap(i + AHEAD, core).start()
        for j in range(X):
            b = (x + j) % X
            t_buf[j * BLOCK : (j + 1) * BLOCK] = lax.dot_general(
                h_buf[...],
                a_buf[i, :, pl.ds(pl.multiple_of(b * BLOCK, BLOCK), BLOCK)],
                (((1,), (1,)), ((), ())),
                preferred_element_type=F32,
            ).astype(BF16)
        m_buf[i] = jnp.dot(t_buf[...], g_buf[...], preferred_element_type=F32).reshape(X, BLOCK, COLS)

    def way_sign(way):
        return 1 - 2 * way

    def z_copy(way, j, k):
        return remote(
            zs.at[way, j, k], zr.at[way, j, k], zssem.at[way, j, k], zrsem.at[way, j, k],
            at_z(way_sign(way)),
        )

    def begins(way, j):
        return j // 2 == way

    def z_step(way, j, k):
        i = STEP[(way_sign(way) * (4 - k)) % Z]
        part = m_buf[i, j, :, 0:128]
        if k >= 2 or (k == 1 and begins(way, j)):
            z_copy(way, j, k - 1).wait_recv()
            part = part + zr[way, j, k - 1].astype(F32)
        zs[way, j, k] = part.astype(BF16)
        z_copy(way, j, k).start()

    def y_copy(way, j, k):
        return remote(
            ys.at[way, j, k], yr.at[way, j, k], yssem.at[way, j, k], yrsem.at[way, j, k],
            at_y(way_sign(way)),
        )

    def y_step(way, j, k):
        first = ((way_sign(way) * (4 - k)) % Y) * SUB
        part = m_buf[:, j, first : first + SUB, 128:256]
        if k >= 2 or (k == 1 and begins(way, j)):
            y_copy(way, j, k - 1).wait_recv()
            part = part + yr[way, j, k - 1].astype(F32)
        ys[way, j, k] = part.astype(BF16)
        y_copy(way, j, k).start()

    def x0_copy(way, i):
        return remote(
            xs0.at[i, way], xr0.at[i, way], x0ssem.at[i, way], x0rsem.at[i, way],
            at_x(way_sign(way)),
        )

    def x1_copy(way, i):
        return remote(
            xs1.at[i, way], xr1.at[i, way], x1ssem.at[i, way], x1rsem.at[i, way],
            at_x(way_sign(way)),
        )

    def v_copy(way, k, h):
        if k == 0:
            src, dst = vs.at[way, 0, h, pl.ds(0, HALF)], vr.at[way, 0, h, pl.ds(0, HALF)]
        else:
            src, dst = vs.at[way, k, h], vr.at[way, k, h]
        return remote(src, dst, vssem.at[way, k, h], vrsem.at[way, k, h], at_z(way_sign(way)))

    def w_copy(j, h):
        return remote(
            v2s.at[h, j - 1], v2r.at[h, j - 1], s2sem.at[2 + h], r2sem.at[2 + h], at_y(j)
        )

    def x0_step(i):
        for way in range(2):
            xs0[i, way] = m_buf[i, 2, way * HALF : (way + 1) * HALF, 256:512].astype(BF16)
            x0_copy(way, i).start()

    def x1_step(i):
        for way in range(2):
            j = 1 + 2 * way
            x0_copy(way, i).wait_recv()
            mine = slice(way * HALF, (way + 1) * HALF)
            rest = slice((1 - way) * HALF, (2 - way) * HALF)
            xs1[i, way, mine] = (m_buf[i, j, mine, 256:512] + xr0[i, way].astype(F32)).astype(BF16)
            xs1[i, way, rest] = m_buf[i, j, rest, 256:512].astype(BF16)
            x1_copy(way, i).start()

    def x2_rows(i, rows, h):
        there = slice(h * 128, (h + 1) * 128)
        return (
            m_buf[i, 0, rows, 256 + h * 128 : 384 + h * 128]
            + xr1[i, 0, rows, there].astype(F32)
            + xr1[i, 1, rows, there].astype(F32)
        )

    def v_step(i, h):
        if i == 0:
            for way in range(2):
                rows = slice(way * HALF, (way + 1) * HALF)
                vs[way, 0, h, 0:HALF] = x2_rows(0, rows, h).astype(BF16)
                v_copy(way, 0, h).start()
            return
        if i < Z - 1:
            way, k = 1 - i % 2, (i + 1) // 2
            v_copy(way, k - 1, h).wait_recv()
            if k == 1:
                mine = slice(way * HALF, (way + 1) * HALF)
                rest = slice((1 - way) * HALF, (2 - way) * HALF)
                vs[way, 1, h, mine] = (
                    x2_rows(i, mine, h) + vr[way, 0, h, 0:HALF].astype(F32)
                ).astype(BF16)
                vs[way, 1, h, rest] = x2_rows(i, rest, h).astype(BF16)
            else:
                vs[way, k, h] = (
                    x2_rows(i, slice(0, BLOCK), h) + vr[way, k - 1, h].astype(F32)
                ).astype(BF16)
            v_copy(way, k, h).start()
            return
        for way in range(2):
            v_copy(way, 3, h).wait_recv()
        part = (
            x2_rows(i, slice(0, BLOCK), h) + vr[0, 3, h].astype(F32) + vr[1, 3, h].astype(F32)
        )
        v_acc[h] = part[0:SUB]
        for j in range(1, Y):
            v2s[h, j - 1] = part[j * SUB : (j + 1) * SUB].astype(BF16)
            w_copy(j, h).start()

    def x1_arrived(i):
        for way in range(2):
            x1_copy(way, i).wait_recv()

    def drain(buf, sem):
        pltpu.make_async_copy(buf, buf, sem).wait()

    def z2_step(j):
        for way in range(2):
            z_copy(way, j, 3).wait_recv()
        part = m_buf[Z - 1, j, :, 0:128] + zr[0, j, 3].astype(F32) + zr[1, j, 3].astype(F32)
        if j == 0:
            z_acc[...] = part
        else:
            z2s[j - 1] = part.astype(BF16)
            remote(z2s.at[j - 1], z2r.at[j - 1], s2sem.at[0], r2sem.at[0], at_x(j)).start()

    def y2_step(j):
        for way in range(2):
            y_copy(way, j, 3).wait_recv()
        part = m_buf[:, j, 0:SUB, 128:256] + yr[0, j, 3].astype(F32) + yr[1, j, 3].astype(F32)
        if j == 0:
            y_acc[...] = part
        else:
            y2s[j - 1] = part.astype(BF16)
            remote(y2s.at[j - 1], y2r.at[j - 1], s2sem.at[1], r2sem.at[1], at_x(j)).start()

    def z3_step():
        drain(z2r, r2sem.at[0])
        part = z_acc[...]
        for q in range(X - 1):
            part = part + z2r[q].astype(F32)
        z_acc[...] = part
        for j in range(1, Y):
            z3s[j - 1] = part[j * SUB : (j + 1) * SUB].astype(BF16)
            remote(z3s.at[j - 1], z3r.at[j - 1], s3sem.at[0], r3sem.at[0], at_y(j)).start()

    def y3_step():
        drain(y2r, r2sem.at[1])
        part = y_acc[...]
        for q in range(X - 1):
            part = part + y2r[q].astype(F32)
        y_acc[...] = part
        for j in range(1, Z):
            y3s[j - 1] = part[STEP[j]].astype(BF16)
            remote(y3s.at[j - 1], y3r.at[j - 1], s3sem.at[1], r3sem.at[1], at_z(j)).start()

    scale = 1.0 / (Z * CORES * X * Y * math.sqrt(BLOCK))

    def finish(own, received, sem, first):
        drain(received, sem)
        total = own
        for q in range(received.shape[0]):
            total = total + received[q].astype(F32)
        out_ref[:, first : first + 128] = total * scale

    g_load.wait()
    g_swap(other).wait_recv()

    compute(0)
    x0_step(0)
    z_step(0, 1, 0)
    compute(1)
    z_step(1, 2, 0)
    z_step(0, 2, 1)
    z_step(1, 3, 0)
    x0_step(1)
    z_step(0, 3, 1)
    z_step(0, 0, 0)
    compute(2)
    compute(3)
    z_step(1, 1, 1)
    x0_step(3)
    z_step(1, 0, 1)
    x0_step(2)
    compute(4)
    x1_step(0)
    compute(5)
    x0_step(4)
    compute(6)
    compute(7)
    y_step(1, 2, 0)
    y_step(0, 2, 1)
    y_step(1, 3, 0)
    x0_step(5)
    z_step(1, 2, 1)
    z_step(1, 3, 1)
    z_step(0, 1, 1)
    y_step(1, 0, 1)
    y_step(1, 1, 1)
    x0_step(6)
    x1_step(2)
    z_step(0, 3, 2)
    x1_step(1)
    z_step(0, 2, 2)
    y_step(0, 1, 0)
    x1_step(3)
    x0_step(7)
    y_step(0, 0, 0)
    x1_arrived(0)
    v_step(0, 0)
    v_step(0, 1)
    z_step(0, 0, 1)
    z_step(1, 0, 2)
    z_step(1, 1, 2)
    y_step(0, 3, 1)
    x1_step(4)
    y_step(1, 2, 1)
    y_step(0, 2, 2)
    z_step(1, 2, 2)
    x1_step(5)
    y_step(1, 3, 1)
    z_step(0, 1, 2)
    z_step(1, 3, 2)
    y_step(1, 0, 2)
    z_step(0, 3, 3)
    x1_step(6)
    y_step(0, 1, 1)
    z_step(0, 2, 3)
    y_step(1, 1, 2)
    x1_arrived(2)
    v_step(2, 0)
    y_step(0, 0, 1)
    v_step(2, 1)
    z_step(1, 0, 3)
    y_step(0, 3, 2)
    y_step(1, 2, 2)
    z_step(0, 0, 2)
    z_step(1, 1, 3)
    x1_arrived(1)
    v_step(1, 0)
    v_step(1, 1)
    y_step(0, 2, 3)
    z_step(0, 1, 3)
    y_step(1, 3, 2)
    z_step(1, 2, 3)
    y_step(1, 0, 3)
    z_step(1, 3, 3)
    y_step(0, 1, 2)
    y_step(1, 1, 3)
    x1_step(7)
    y_step(0, 0, 2)
    y_step(0, 3, 3)
    y_step(1, 2, 3)
    z_step(0, 0, 3)
    x1_arrived(4)
    v_step(4, 1)
    v_step(4, 0)
    x1_arrived(3)
    v_step(3, 0)
    y_step(1, 3, 3)
    v_step(3, 1)
    z2_step(2)
    y_step(0, 1, 3)
    z2_step(1)
    z2_step(3)
    y_step(0, 0, 3)
    y2_step(2)
    z2_step(0)
    x1_arrived(6)
    v_step(6, 1)
    x1_arrived(5)
    v_step(5, 0)
    y2_step(3)
    v_step(6, 0)
    v_step(5, 1)
    y2_step(1)
    y2_step(0)
    z3_step()
    x1_arrived(7)
    v_step(7, 0)
    v_step(7, 1)
    y3_step()
    finish(z_acc[0:SUB], z3r, r3sem.at[0], 0)
    finish(v_acc[0], v2r.at[0], r2sem.at[2], 256)
    finish(v_acc[1], v2r.at[1], r2sem.at[3], 384)
    finish(y_acc[Z - 1], y3r, r3sem.at[1], 128)

    g_swap(core).wait_send()

    @pl.loop(0, Z)
    def _(i):
        swap(i, core).wait_send()
        for way in range(2):
            x0_copy(way, i).wait_send()
            x1_copy(way, i).wait_send()

    for way in range(2):
        for k in range(4):
            for h in range(2):
                v_copy(way, k, h).wait_send()
            for j in range(X):
                if k > 0 or begins(way, j):
                    z_copy(way, j, k).wait_send()
                    y_copy(way, j, k).wait_send()
    for at, buf in enumerate((z2s, y2s, v2s.at[0], v2s.at[1])):
        drain(buf, s2sem.at[at])
    for at, buf in enumerate((z3s, y3s)):
        drain(buf, s3sem.at[at])


def per_device(activations, out_grads):
    def vm(*shape, dtype=BF16):
        return pltpu.VMEM(shape, dtype)

    dma = pltpu.SemaphoreType.DMA
    scratch = [
        vm(Z, CORES * TOK, WIDTH), vm(CORES * TOK, COLS), vm(BLOCK, BLOCK), vm(WIDTH, CORES * TOK),
        vm(Z, X, BLOCK, COLS, dtype=F32),
        vm(2, X, 4, BLOCK, 128), vm(2, X, 4, BLOCK, 128),
        vm(2, X, 4, Z, SUB, 128), vm(2, X, 4, Z, SUB, 128),
        vm(Z, 2, HALF, 256), vm(Z, 2, HALF, 256),
        vm(Z, 2, BLOCK, 256), vm(Z, 2, BLOCK, 256),
        vm(2, 4, 2, BLOCK, 128), vm(2, 4, 2, BLOCK, 128),
        vm(X - 1, BLOCK, 128), vm(X - 1, BLOCK, 128),
        vm(X - 1, Z, SUB, 128), vm(X - 1, Z, SUB, 128),
        vm(2, Y - 1, SUB, 128), vm(2, Y - 1, SUB, 128),
        vm(Y - 1, SUB, 128), vm(Y - 1, SUB, 128),
        vm(Z - 1, SUB, 128), vm(Z - 1, SUB, 128),
        vm(BLOCK, 128, dtype=F32), vm(Z, SUB, 128, dtype=F32), vm(2, SUB, 128, dtype=F32),
        dma((Z,)), dma, dma((Z,)), dma((Z,)), dma, dma,
        dma((2, X, 4)), dma((2, X, 4)), dma((2, X, 4)), dma((2, X, 4)),
        dma((Z, 2)), dma((Z, 2)), dma((Z, 2)), dma((Z, 2)), dma((2, 4, 2)), dma((2, 4, 2)),
        dma((4,)), dma((4,)), dma((2,)), dma((2,)),
    ]
    return pl.pallas_call(
        kernel,
        out_shape=jax.ShapeDtypeStruct((SUB, COLS), F32),
        in_specs=[pl.BlockSpec(memory_space=pl.ANY)] * 2,
        out_specs=pl.BlockSpec(memory_space=pltpu.VMEM),
        scratch_shapes=scratch,
        compiler_params=pltpu.CompilerParams(
            collective_id=0, has_side_effects=True, vmem_limit_bytes=60 * 1024 * 1024
        ),
        cost_estimate=pl.CostEstimate(
            flops=2 * CORES * TOK * Z * WIDTH * (COLS + BLOCK),
            bytes_accessed=TOK * (2 * Z * WIDTH + COLS) * 2,
            transcendentals=0,
        ),
    )(activations, out_grads)


def solution(mesh):
    return jax.shard_map(
        per_device,
        mesh=mesh,
        in_specs=(P(("narrow", "wide"), None), P(("narrow", "wide"), None)),
        out_specs=P(("narrow", "wide"), None),
        check_vma=False,
    )
```

time: 55.8 us -> 48.9 us (0.88)
  Pallas kernels: 54.2 us -> 47.1 us
    pallas_call x1, Pallas kernels: 54.2 us -> 47.1 us  [per_device(): pl.pallas_call(kernel, out_shape=jax.ShapeDtypeStruct((SUB, COLS), F32),...]
where the time goes in v3:
time: 48.9 us; the launch traced here: 48.5 us
  Pallas kernels  47.1 us (96%)
  local copies, waits for them, and re-layouts  1.38 us (3%)
    pallas_call x1, Pallas kernels, per_device(): pl.pallas_call(kernel, out_shape=jax.ShapeDtypeStruct((SUB, COLS), F32),...  47.1 us
    unnamed x1, local copies, waits for them, and re-layouts  1.38 us

profile of v3, /device:TPU:8, one launch (start us, length us, event | category | flops | bytes accessed | tf_op | source)
XLA Modules:
  0.0 48.5 jit_solution(13542093897371967232)
XLA Ops:
  0.0 47.1 %shard_map.28 = f32[16,512]{1,0:T(8,128)} custom-call(bf16[256,8192]{1,0:T(8,128)(2,1)} %act_ref.1, bf16[256,512]{1,0:T(8,128)(2,1)} %grad_ref.1), custom_call_target="tpu_custom_call" | custom-call | flops 2684354560 | bytes 4456448 | tf_op jit(solution)/shard_map/pallas_call | solution.py:466
  47.1 1.4 %copy.4 = f32[16,512]{1,0:T(8,128)} copy(f32[16,512]{1,0:T(8,128)} %shard_map.28) | data formatting | bytes 65536

commit v4 on v3

--- a/solution.py
+++ b/solution.py
@@ -25,11 +25,11 @@
 def kernel(
     act_ref, grad_ref, out_ref,
     a_buf, g_buf, h_buf, t_buf, m_buf,
-    zs, zr, ys, yr, xs0, xr0, xs1, xr1, vs, vr,
+    zs, zr, ys, yr, xs0, xr0, xs1, xr1, vs0, vr0, vs, vr,
     z2s, z2r, y2s, y2r, v2s, v2r, z3s, z3r, y3s, y3r,
     z_acc, y_acc, v_acc,
     load_sem, gload_sem, asend, arecv, gsend, grecv,
-    zssem, zrsem, yssem, yrsem, x0ssem, x0rsem, x1ssem, x1rsem, vssem, vrsem,
+    zssem, zrsem, yssem, yrsem, x0ssem, x0rsem, x1ssem, x1rsem, v0ssem, vssem, vrsem,
     s2sem, r2sem, s3sem, r3sem,
 ):
     n = lax.axis_index("narrow")
@@ -55,6 +55,9 @@
             device_id=target, device_id_type=MESH,
         )
 
+    def drain(buf, sem):
+        pltpu.make_async_copy(buf, buf, sem).wait()
+
     def place(i):
         return (z + 4 + i // 2 - (i % 2) * i + 2 * Z) % Z
 
@@ -62,14 +65,14 @@
         return pltpu.make_async_copy(
             act_ref.at[:, pl.ds((place(i) * CORES + core) * WIDTH, WIDTH)],
             a_buf.at[i, pl.ds(core * TOK, TOK), :],
-            load_sem.at[i],
+            load_sem,
         )
 
     def swap(i, half):
         return remote(
             act_ref.at[:, pl.ds((place(i) * CORES + other) * WIDTH, WIDTH)],
             a_buf.at[i, pl.ds(half * TOK, TOK), :],
-            asend.at[i], arecv.at[i], sibling,
+            asend, arecv.at[i], sibling,
         )
 
     def g_swap(half):
@@ -108,7 +111,6 @@
         swap(i, core).start()
 
     def compute(i):
-        own_load(i).wait()
         swap(i, other).wait_recv()
         if i + AHEAD < Z:
             swap(i + AHEAD, core).start()
@@ -125,9 +127,19 @@
     def way_sign(way):
         return 1 - 2 * way
 
+    def slot(way, j, k):
+        if k == 0:
+            return 24 + 2 * way + j % 2
+        if k == 3:
+            return 16 + 2 * j + way
+        return 8 * (k - 1) + 4 * way + j
+
+    def mark(way, j, k):
+        return 16 + j if k == 3 else slot(way, j, k) - 4 * (k == 0)
+
     def z_copy(way, j, k):
         return remote(
-            zs.at[way, j, k], zr.at[way, j, k], zssem.at[way, j, k], zrsem.at[way, j, k],
+            zs.at[slot(way, j, k)], zr.at[slot(way, j, k)], zssem, zrsem.at[mark(way, j, k)],
             at_z(way_sign(way)),
         )
 
@@ -139,13 +151,13 @@
         part = m_buf[i, j, :, 0:128]
         if k >= 2 or (k == 1 and begins(way, j)):
             z_copy(way, j, k - 1).wait_recv()
-            part = part + zr[way, j, k - 1].astype(F32)
-        zs[way, j, k] = part.astype(BF16)
+            part = part + zr[slot(way, j, k - 1)].astype(F32)
+        zs[slot(way, j, k)] = part.astype(BF16)
         z_copy(way, j, k).start()
 
     def y_copy(way, j, k):
         return remote(
-            ys.at[way, j, k], yr.at[way, j, k], yssem.at[way, j, k], yrsem.at[way, j, k],
+            ys.at[slot(way, j, k)], yr.at[slot(way, j, k)], yssem, yrsem.at[mark(way, j, k)],
             at_y(way_sign(way)),
         )
 
@@ -154,28 +166,32 @@
         part = m_buf[:, j, first : first + SUB, 128:256]
         if k >= 2 or (k == 1 and begins(way, j)):
             y_copy(way, j, k - 1).wait_recv()
-            part = part + yr[way, j, k - 1].astype(F32)
-        ys[way, j, k] = part.astype(BF16)
+            part = part + yr[slot(way, j, k - 1)].astype(F32)
+        ys[slot(way, j, k)] = part.astype(BF16)
         y_copy(way, j, k).start()
 
     def x0_copy(way, i):
         return remote(
-            xs0.at[i, way], xr0.at[i, way], x0ssem.at[i, way], x0rsem.at[i, way],
+            xs0.at[i, way], xr0.at[i, way], x0ssem, x0rsem.at[i],
             at_x(way_sign(way)),
         )
 
     def x1_copy(way, i):
         return remote(
-            xs1.at[i, way], xr1.at[i, way], x1ssem.at[i, way], x1rsem.at[i, way],
+            xs1.at[i, way], xr1.at[i, way], x1ssem, x1rsem.at[i],
             at_x(way_sign(way)),
         )
+
+    def v_slot(way, k, h):
+        return 8 + 2 * h + way if k == 3 else 4 * (k - 1) + 2 * way + h
 
     def v_copy(way, k, h):
         if k == 0:
-            src, dst = vs.at[way, 0, h, pl.ds(0, HALF)], vr.at[way, 0, h, pl.ds(0, HALF)]
+            src, dst, ssem, mine = vs0.at[way, h], vr0.at[way, h], v0ssem, 10 + 2 * way + h
         else:
-            src, dst = vs.at[way, k, h], vr.at[way, k, h]
-        return remote(src, dst, vssem.at[way, k, h], vrsem.at[way, k, h], at_z(way_sign(way)))
+            at = v_slot(way, k, h)
+            src, dst, ssem, mine = vs.at[at], vr.at[at], vssem, 8 + h if k == 3 else at
+        return remote(src, dst, ssem, vrsem.at[mine], at_z(way_sign(way)))
 
     def w_copy(j, h):
         return remote(
@@ -188,9 +204,9 @@
             x0_copy(way, i).start()
 
     def x1_step(i):
+        drain(xr0.at[i], x0rsem.at[i])
         for way in range(2):
             j = 1 + 2 * way
-            x0_copy(way, i).wait_recv()
             mine = slice(way * HALF, (way + 1) * HALF)
             rest = slice((1 - way) * HALF, (2 - way) * HALF)
             xs1[i, way, mine] = (m_buf[i, j, mine, 256:512] + xr0[i, way].astype(F32)).astype(BF16)
@@ -209,7 +225,7 @@
         if i == 0:
             for way in range(2):
                 rows = slice(way * HALF, (way + 1) * HALF)
-                vs[way, 0, h, 0:HALF] = x2_rows(0, rows, h).astype(BF16)
+                vs0[way, h] = x2_rows(0, rows, h).astype(BF16)
                 v_copy(way, 0, h).start()
             return
         if i < Z - 1:
@@ -218,20 +234,19 @@
             if k == 1:
                 mine = slice(way * HALF, (way + 1) * HALF)
                 rest = slice((1 - way) * HALF, (2 - way) * HALF)
-                vs[way, 1, h, mine] = (
-                    x2_rows(i, mine, h) + vr[way, 0, h, 0:HALF].astype(F32)
+                vs[v_slot(way, 1, h), mine] = (
+                    x2_rows(i, mine, h) + vr0[way, h].astype(F32)
                 ).astype(BF16)
-                vs[way, 1, h, rest] = x2_rows(i, rest, h).astype(BF16)
+                vs[v_slot(way, 1, h), rest] = x2_rows(i, rest, h).astype(BF16)
             else:
-                vs[way, k, h] = (
-                    x2_rows(i, slice(0, BLOCK), h) + vr[way, k - 1, h].astype(F32)
+                vs[v_slot(way, k, h)] = (
+                    x2_rows(i, slice(0, BLOCK), h) + vr[v_slot(way, k - 1, h)].astype(F32)
                 ).astype(BF16)
             v_copy(way, k, h).start()
             return
-        for way in range(2):
-            v_copy(way, 3, h).wait_recv()
+        drain(vr.at[pl.ds(8 + 2 * h, 2)], vrsem.at[8 + h])
         part = (
-            x2_rows(i, slice(0, BLOCK), h) + vr[0, 3, h].astype(F32) + vr[1, 3, h].astype(F32)
+            x2_rows(i, slice(0, BLOCK), h) + vr[8 + 2 * h].astype(F32) + vr[9 + 2 * h].astype(F32)
         )
         v_acc[h] = part[0:SUB]
         for j in range(1, Y):
@@ -239,16 +254,11 @@
             w_copy(j, h).start()
 
     def x1_arrived(i):
-        for way in range(2):
-            x1_copy(way, i).wait_recv()
-
-    def drain(buf, sem):
-        pltpu.make_async_copy(buf, buf, sem).wait()
+        drain(xr1.at[i], x1rsem.at[i])
 
     def z2_step(j):
-        for way in range(2):
-            z_copy(way, j, 3).wait_recv()
-        part = m_buf[Z - 1, j, :, 0:128] + zr[0, j, 3].astype(F32) + zr[1, j, 3].astype(F32)
+        drain(zr.at[pl.ds(slot(0, j, 3), 2)], zrsem.at[mark(0, j, 3)])
+        part = m_buf[Z - 1, j, :, 0:128] + zr[slot(0, j, 3)].astype(F32) + zr[slot(1, j, 3)].astype(F32)
         if j == 0:
             z_acc[...] = part
         else:
@@ -256,9 +266,8 @@
             remote(z2s.at[j - 1], z2r.at[j - 1], s2sem.at[0], r2sem.at[0], at_x(j)).start()
 
     def y2_step(j):
-        for way in range(2):
-            y_copy(way, j, 3).wait_recv()
-        part = m_buf[:, j, 0:SUB, 128:256] + yr[0, j, 3].astype(F32) + yr[1, j, 3].astype(F32)
+        drain(yr.at[pl.ds(slot(0, j, 3), 2)], yrsem.at[mark(0, j, 3)])
+        part = m_buf[:, j, 0:SUB, 128:256] + yr[slot(0, j, 3)].astype(F32) + yr[slot(1, j, 3)].astype(F32)
         if j == 0:
             y_acc[...] = part
         else:
@@ -295,144 +304,135 @@
         out_ref[:, first : first + 128] = total * scale
 
     g_load.wait()
+    drain(a_buf.at[:, pl.ds(core * TOK, TOK), :], load_sem)
     g_swap(other).wait_recv()
 
     compute(0)
     x0_step(0)
+    compute(1)
+    x0_step(1)
+    compute(2)
+    x0_step(2)
+    z_step(1, 2, 0)
+    compute(3)
+    x0_step(3)
     z_step(0, 1, 0)
-    compute(1)
-    z_step(1, 2, 0)
+    z_step(1, 3, 0)
+    compute(4)
+    x0_step(4)
+    compute(5)
     z_step(0, 2, 1)
-    z_step(1, 3, 0)
-    x0_step(1)
-    z_step(0, 3, 1)
-    z_step(0, 0, 0)
-    compute(2)
-    compute(3)
-    z_step(1, 1, 1)
-    x0_step(3)
-    z_step(1, 0, 1)
-    x0_step(2)
-    compute(4)
+    x0_step(5)
+    compute(6)
     x1_step(0)
-    compute(5)
-    x0_step(4)
-    compute(6)
     compute(7)
     y_step(1, 2, 0)
+    y_step(0, 1, 0)
+    z_step(0, 3, 1)
+    z_step(1, 1, 1)
+    y_step(0, 0, 0)
+    x1_step(1)
+    y_step(0, 3, 1)
+    y_step(1, 3, 0)
+    z_step(1, 2, 1)
+    y_step(1, 1, 1)
+    z_step(0, 0, 0)
+    x1_step(2)
+    z_step(0, 1, 1)
+    z_step(1, 3, 1)
+    x0_step(6)
+    z_step(1, 0, 1)
     y_step(0, 2, 1)
-    y_step(1, 3, 0)
-    x0_step(5)
-    z_step(1, 2, 1)
-    z_step(1, 3, 1)
-    z_step(0, 1, 1)
+    z_step(0, 2, 2)
     y_step(1, 0, 1)
-    y_step(1, 1, 1)
-    x0_step(6)
-    x1_step(2)
+    x0_step(7)
+    y_step(1, 2, 1)
+    x1_arrived(0)
+    v_step(0, 1)
+    v_step(0, 0)
+    y_step(0, 1, 1)
     z_step(0, 3, 2)
-    x1_step(1)
-    z_step(0, 2, 2)
-    y_step(0, 1, 0)
-    x1_step(3)
-    x0_step(7)
-    y_step(0, 0, 0)
-    x1_arrived(0)
-    v_step(0, 0)
-    v_step(0, 1)
+    z_step(1, 1, 2)
+    y_step(1, 3, 1)
+    z_step(1, 2, 2)
     z_step(0, 0, 1)
-    z_step(1, 0, 2)
-    z_step(1, 1, 2)
-    y_step(0, 3, 1)
     x1_step(4)
-    y_step(1, 2, 1)
-    y_step(0, 2, 2)
-    z_step(1, 2, 2)
-    x1_step(5)
-    y_step(1, 3, 1)
+    y_step(0, 0, 1)
+    y_step(1, 1, 2)
     z_step(0, 1, 2)
     z_step(1, 3, 2)
+    y_step(0, 3, 2)
+    y_step(0, 2, 2)
+    x1_step(3)
+    z_step(0, 2, 3)
+    z_step(1, 0, 2)
+    x1_arrived(1)
+    v_step(1, 1)
+    x1_arrived(2)
+    v_step(2, 1)
+    y_step(1, 2, 2)
+    v_step(2, 0)
+    x1_step(5)
+    v_step(1, 0)
+    y_step(0, 1, 2)
+    y_step(1, 3, 2)
+    z_step(0, 3, 3)
+    z_step(1, 2, 3)
     y_step(1, 0, 2)
-    z_step(0, 3, 3)
-    x1_step(6)
-    y_step(0, 1, 1)
-    z_step(0, 2, 3)
-    y_step(1, 1, 2)
-    x1_arrived(2)
-    v_step(2, 0)
-    y_step(0, 0, 1)
-    v_step(2, 1)
-    z_step(1, 0, 3)
-    y_step(0, 3, 2)
-    y_step(1, 2, 2)
     z_step(0, 0, 2)
     z_step(1, 1, 3)
-    x1_arrived(1)
-    v_step(1, 0)
-    v_step(1, 1)
+    x1_step(6)
+    z_step(1, 3, 3)
+    z_step(0, 1, 3)
+    y_step(1, 1, 3)
+    y_step(0, 3, 3)
+    x1_step(7)
     y_step(0, 2, 3)
-    z_step(0, 1, 3)
-    y_step(1, 3, 2)
-    z_step(1, 2, 3)
-    y_step(1, 0, 3)
-    z_step(1, 3, 3)
-    y_step(0, 1, 2)
-    y_step(1, 1, 3)
-    x1_step(7)
-    y_step(0, 0, 2)
-    y_step(0, 3, 3)
     y_step(1, 2, 3)
-    z_step(0, 0, 3)
+    x1_arrived(3)
+    v_step(3, 1)
     x1_arrived(4)
     v_step(4, 1)
+    y_step(0, 0, 2)
     v_step(4, 0)
-    x1_arrived(3)
     v_step(3, 0)
+    y_step(0, 1, 3)
     y_step(1, 3, 3)
-    v_step(3, 1)
     z2_step(2)
-    y_step(0, 1, 3)
+    z_step(1, 0, 3)
+    z_step(0, 0, 3)
     z2_step(1)
     z2_step(3)
-    y_step(0, 0, 3)
+    y_step(1, 0, 3)
     y2_step(2)
-    z2_step(0)
+    x1_arrived(5)
+    v_step(5, 1)
     x1_arrived(6)
     v_step(6, 1)
-    x1_arrived(5)
     v_step(5, 0)
+    y_step(0, 0, 3)
+    v_step(6, 0)
+    y2_step(1)
     y2_step(3)
-    v_step(6, 0)
-    v_step(5, 1)
-    y2_step(1)
-    y2_step(0)
+    z2_step(0)
     z3_step()
     x1_arrived(7)
+    v_step(7, 1)
+    y2_step(0)
     v_step(7, 0)
-    v_step(7, 1)
     y3_step()
     finish(z_acc[0:SUB], z3r, r3sem.at[0], 0)
+    finish(y_acc[Z - 1], y3r, r3sem.at[1], 128)
     finish(v_acc[0], v2r.at[0], r2sem.at[2], 256)
     finish(v_acc[1], v2r.at[1], r2sem.at[3], 384)
-    finish(y_acc[Z - 1], y3r, r3sem.at[1], 128)
 
     g_swap(core).wait_send()
 
-    @pl.loop(0, Z)
-    def _(i):
-        swap(i, core).wait_send()
-        for way in range(2):
-            x0_copy(way, i).wait_send()
-            x1_copy(way, i).wait_send()
-
-    for way in range(2):
-        for k in range(4):
-            for h in range(2):
-                v_copy(way, k, h).wait_send()
-            for j in range(X):
-                if k > 0 or begins(way, j):
-                    z_copy(way, j, k).wait_send()
-                    y_copy(way, j, k).wait_send()
+    drain(a_buf.at[:, pl.ds(0, TOK), :], asend)
+    for buf, sem in (
+        (zs, zssem), (ys, yssem), (xs0, x0ssem), (xs1, x1ssem), (vs0, v0ssem), (vs, vssem)
+    ):
+        drain(buf, sem)
     for at, buf in enumerate((z2s, y2s, v2s.at[0], v2s.at[1])):
         drain(buf, s2sem.at[at])
     for at, buf in enumerate((z3s, y3s)):
@@ -447,20 +447,21 @@
     scratch = [
         vm(Z, CORES * TOK, WIDTH), vm(CORES * TOK, COLS), vm(BLOCK, BLOCK), vm(WIDTH, CORES * TOK),
         vm(Z, X, BLOCK, COLS, dtype=F32),
-        vm(2, X, 4, BLOCK, 128), vm(2, X, 4, BLOCK, 128),
-        vm(2, X, 4, Z, SUB, 128), vm(2, X, 4, Z, SUB, 128),
+        vm(28, BLOCK, 128), vm(28, BLOCK, 128),
+        vm(28, Z, SUB, 128), vm(28, Z, SUB, 128),
         vm(Z, 2, HALF, 256), vm(Z, 2, HALF, 256),
         vm(Z, 2, BLOCK, 256), vm(Z, 2, BLOCK, 256),
-        vm(2, 4, 2, BLOCK, 128), vm(2, 4, 2, BLOCK, 128),
+        vm(2, 2, HALF, 128), vm(2, 2, HALF, 128),
+        vm(12, BLOCK, 128), vm(12, BLOCK, 128),
         vm(X - 1, BLOCK, 128), vm(X - 1, BLOCK, 128),
         vm(X - 1, Z, SUB, 128), vm(X - 1, Z, SUB, 128),
         vm(2, Y - 1, SUB, 128), vm(2, Y - 1, SUB, 128),
         vm(Y - 1, SUB, 128), vm(Y - 1, SUB, 128),
         vm(Z - 1, SUB, 128), vm(Z - 1, SUB, 128),
         vm(BLOCK, 128, dtype=F32), vm(Z, SUB, 128, dtype=F32), vm(2, SUB, 128, dtype=F32),
-        dma((Z,)), dma, dma((Z,)), dma((Z,)), dma, dma,
-        dma((2, X, 4)), dma((2, X, 4)), dma((2, X, 4)), dma((2, X, 4)),
-        dma((Z, 2)), dma((Z, 2)), dma((Z, 2)), dma((Z, 2)), dma((2, 4, 2)), dma((2, 4, 2)),
+        dma, dma, dma, dma((Z,)), dma, dma,
+        dma, dma((24,)), dma, dma((24,)),
+        dma, dma((Z,)), dma, dma((Z,)), dma, dma, dma((14,)),
         dma((4,)), dma((4,)), dma((2,)), dma((2,)),
     ]
     return pl.pallas_call(

time: 48.9 us -> 46.7 us (0.955)
  Pallas kernels: 47.1 us -> 45.1 us
    pallas_call x1, Pallas kernels: 47.1 us -> 45.1 us  [per_device(): pl.pallas_call(kernel, out_shape=jax.ShapeDtypeStruct((SUB, COLS), F32),...]
where the time goes in v4:
time: 46.7 us; the launch traced here: 46.5 us
  Pallas kernels  45.1 us (97%)
  local copies, waits for them, and re-layouts  1.38 us (3%)
    pallas_call x1, Pallas kernels, per_device(): pl.pallas_call(kernel, out_shape=jax.ShapeDtypeStruct((SUB, COLS), F32),...  45.1 us
    unnamed x1, local copies, waits for them, and re-layouts  1.38 us

profile of v4, /device:TPU:8, one launch (start us, length us, event | category | flops | bytes accessed | tf_op | source)
XLA Modules:
  0.0 46.5 jit_solution(6685200240496952466)
XLA Ops:
  0.0 45.1 %shard_map.28 = f32[16,512]{1,0:T(8,128)} custom-call(bf16[256,8192]{1,0:T(8,128)(2,1)} %act_ref.1, bf16[256,512]{1,0:T(8,128)(2,1)} %grad_ref.1), custom_call_target="tpu_custom_call" | custom-call | flops 2684354560 | bytes 4456448 | tf_op jit(solution)/shard_map/pallas_call | solution.py:467
  45.1 1.4 %copy.4 = f32[16,512]{1,0:T(8,128)} copy(f32[16,512]{1,0:T(8,128)} %shard_map.28) | data formatting | bytes 65536

commit v5 on v4

--- a/solution.py
+++ b/solution.py
@@ -72,11 +72,25 @@
         return remote(
             act_ref.at[:, pl.ds((place(i) * CORES + other) * WIDTH, WIDTH)],
             a_buf.at[i, pl.ds(half * TOK, TOK), :],
-            asend, arecv.at[i], sibling,
-        )
-
-    def g_swap(half):
-        return remote(grad_ref, g_buf.at[pl.ds(half * TOK, TOK), :], gsend, grecv, sibling)
+            asend, arecv.at[i + X - 1], sibling,
+        )
+
+    def columns(j):
+        return pl.multiple_of((x + j) % X * BLOCK, BLOCK)
+
+    def first_swap(j, half):
+        return remote(
+            act_ref.at[:, pl.ds((place(0) * CORES + other) * WIDTH + columns(j), BLOCK)],
+            a_buf.at[0, pl.ds(half * TOK, TOK), pl.ds(columns(j), BLOCK)],
+            asend, arecv.at[j], sibling,
+        )
+
+    def g_swap(part, half):
+        there = pl.ds(part * (COLS // 2), COLS // 2)
+        return remote(
+            grad_ref.at[:, there], g_buf.at[pl.ds(half * TOK, TOK), there],
+            gsend, grecv.at[part], sibling,
+        )
 
     g_load = pltpu.make_async_copy(grad_ref, g_buf.at[pl.ds(core * TOK, TOK), :], gload_sem)
 
@@ -105,23 +119,43 @@
 
     pl.semaphore_wait(barrier, 1 + (Z - 1) + (Y - 1) + (X - 1))
 
-    g_swap(core).start()
-
-    for i in range(AHEAD):
+    g_swap(1, core).start()
+    for j in (2, 0, 1, 3):
+        first_swap(j, core).start()
+    g_swap(0, core).start()
+    for i in range(1, AHEAD):
         swap(i, core).start()
 
+    def turn(i, j):
+        t_buf[j * BLOCK : (j + 1) * BLOCK] = lax.dot_general(
+            h_buf[...],
+            a_buf[i, :, pl.ds(columns(j), BLOCK)],
+            (((1,), (1,)), ((), ())),
+            preferred_element_type=F32,
+        ).astype(BF16)
+
+    def compute_first():
+        g_load.wait()
+        drain(a_buf.at[:, pl.ds(core * TOK, TOK), :], load_sem)
+        g_swap(1, other).wait_recv()
+        first_swap(2, other).wait_recv()
+        turn(0, 2)
+        m_buf[0, 2, :, 256:512] = jnp.dot(
+            t_buf[2 * BLOCK : 3 * BLOCK], g_buf[:, 256:512], preferred_element_type=F32
+        )
+
     def compute(i):
-        swap(i, other).wait_recv()
+        if i == 0:
+            for j in (0, 1, 3):
+                first_swap(j, other).wait_recv()
+            g_swap(0, other).wait_recv()
+        else:
+            swap(i, other).wait_recv()
         if i + AHEAD < Z:
             swap(i + AHEAD, core).start()
         for j in range(X):
-            b = (x + j) % X
-            t_buf[j * BLOCK : (j + 1) * BLOCK] = lax.dot_general(
-                h_buf[...],
-                a_buf[i, :, pl.ds(pl.multiple_of(b * BLOCK, BLOCK), BLOCK)],
-                (((1,), (1,)), ((), ())),
-                preferred_element_type=F32,
-            ).astype(BF16)
+            if i > 0 or j != 2:
+                turn(i, j)
         m_buf[i] = jnp.dot(t_buf[...], g_buf[...], preferred_element_type=F32).reshape(X, BLOCK, COLS)
 
     def way_sign(way):
@@ -249,7 +283,7 @@
             x2_rows(i, slice(0, BLOCK), h) + vr[8 + 2 * h].astype(F32) + vr[9 + 2 * h].astype(F32)
         )
         v_acc[h] = part[0:SUB]
-        for j in range(1, Y):
+        for j in OFFSET[:-1]:
             v2s[h, j - 1] = part[j * SUB : (j + 1) * SUB].astype(BF16)
             w_copy(j, h).start()
 
@@ -280,7 +314,7 @@
         for q in range(X - 1):
             part = part + z2r[q].astype(F32)
         z_acc[...] = part
-        for j in range(1, Y):
+        for j in OFFSET[:-1]:
             z3s[j - 1] = part[j * SUB : (j + 1) * SUB].astype(BF16)
             remote(z3s.at[j - 1], z3r.at[j - 1], s3sem.at[0], r3sem.at[0], at_y(j)).start()
 
@@ -290,7 +324,7 @@
         for q in range(X - 1):
             part = part + y2r[q].astype(F32)
         y_acc[...] = part
-        for j in range(1, Z):
+        for j in OFFSET[:-1]:
             y3s[j - 1] = part[STEP[j]].astype(BF16)
             remote(y3s.at[j - 1], y3r.at[j - 1], s3sem.at[1], r3sem.at[1], at_z(j)).start()
 
@@ -303,12 +337,10 @@
             total = total + received[q].astype(F32)
         out_ref[:, first : first + 128] = total * scale
 
-    g_load.wait()
-    drain(a_buf.at[:, pl.ds(core * TOK, TOK), :], load_sem)
-    g_swap(other).wait_recv()
-
+
+    compute_first()
+    x0_step(0)
     compute(0)
-    x0_step(0)
     compute(1)
     x0_step(1)
     compute(2)
@@ -317,116 +349,116 @@
     compute(3)
     x0_step(3)
     z_step(0, 1, 0)
-    z_step(1, 3, 0)
     compute(4)
     x0_step(4)
+    z_step(1, 3, 0)
+    x1_step(0)
     compute(5)
-    z_step(0, 2, 1)
-    x0_step(5)
     compute(6)
-    x1_step(0)
     compute(7)
     y_step(1, 2, 0)
+    x0_step(6)
+    z_step(0, 0, 0)
     y_step(0, 1, 0)
-    z_step(0, 3, 1)
     z_step(1, 1, 1)
+    y_step(1, 3, 0)
+    x1_step(2)
+    z_step(0, 2, 1)
+    y_step(1, 1, 1)
+    z_step(1, 2, 1)
     y_step(0, 0, 0)
-    x1_step(1)
-    y_step(0, 3, 1)
-    y_step(1, 3, 0)
-    z_step(1, 2, 1)
-    y_step(1, 1, 1)
-    z_step(0, 0, 0)
-    x1_step(2)
-    z_step(0, 1, 1)
-    z_step(1, 3, 1)
-    x0_step(6)
     z_step(1, 0, 1)
     y_step(0, 2, 1)
-    z_step(0, 2, 2)
+    z_step(0, 1, 1)
     y_step(1, 0, 1)
-    x0_step(7)
-    y_step(1, 2, 1)
+    z_step(1, 3, 1)
+    x1_step(1)
+    x0_step(5)
+    z_step(0, 3, 1)
+    y_step(0, 3, 1)
+    x1_step(4)
     x1_arrived(0)
     v_step(0, 1)
     v_step(0, 0)
+    x0_step(7)
+    y_step(1, 2, 1)
+    z_step(0, 0, 1)
+    z_step(1, 1, 2)
     y_step(0, 1, 1)
-    z_step(0, 3, 2)
-    z_step(1, 1, 2)
     y_step(1, 3, 1)
+    z_step(0, 2, 2)
     z_step(1, 2, 2)
-    z_step(0, 0, 1)
-    x1_step(4)
-    y_step(0, 0, 1)
+    x1_step(3)
     y_step(1, 1, 2)
     z_step(0, 1, 2)
+    z_step(1, 0, 2)
+    y_step(0, 0, 1)
+    y_step(0, 2, 2)
+    z_step(0, 3, 2)
+    x1_step(6)
     z_step(1, 3, 2)
-    y_step(0, 3, 2)
-    y_step(0, 2, 2)
-    x1_step(3)
-    z_step(0, 2, 3)
-    z_step(1, 0, 2)
-    x1_arrived(1)
-    v_step(1, 1)
+    y_step(1, 0, 2)
     x1_arrived(2)
     v_step(2, 1)
+    x1_arrived(1)
+    v_step(1, 0)
     y_step(1, 2, 2)
+    v_step(1, 1)
     v_step(2, 0)
     x1_step(5)
-    v_step(1, 0)
+    y_step(0, 3, 2)
+    y_step(1, 3, 2)
+    z_step(0, 2, 3)
     y_step(0, 1, 2)
-    y_step(1, 3, 2)
+    z_step(1, 2, 3)
+    z_step(0, 1, 3)
+    z_step(1, 1, 3)
+    y_step(1, 1, 3)
+    y_step(0, 0, 2)
+    z_step(0, 0, 2)
     z_step(0, 3, 3)
-    z_step(1, 2, 3)
-    y_step(1, 0, 2)
-    z_step(0, 0, 2)
-    z_step(1, 1, 3)
-    x1_step(6)
     z_step(1, 3, 3)
-    z_step(0, 1, 3)
-    y_step(1, 1, 3)
-    y_step(0, 3, 3)
+    y_step(0, 2, 3)
     x1_step(7)
-    y_step(0, 2, 3)
+    x1_arrived(4)
+    v_step(4, 1)
     y_step(1, 2, 3)
     x1_arrived(3)
     v_step(3, 1)
-    x1_arrived(4)
-    v_step(4, 1)
-    y_step(0, 0, 2)
+    v_step(3, 0)
+    y_step(0, 3, 3)
     v_step(4, 0)
-    v_step(3, 0)
+    y_step(1, 3, 3)
+    y_step(1, 0, 3)
     y_step(0, 1, 3)
-    y_step(1, 3, 3)
     z2_step(2)
+    z2_step(1)
     z_step(1, 0, 3)
+    y_step(0, 0, 3)
     z_step(0, 0, 3)
-    z2_step(1)
     z2_step(3)
-    y_step(1, 0, 3)
+    x1_arrived(6)
+    v_step(6, 1)
     y2_step(2)
     x1_arrived(5)
     v_step(5, 1)
-    x1_arrived(6)
-    v_step(6, 1)
+    v_step(6, 0)
+    y2_step(3)
     v_step(5, 0)
-    y_step(0, 0, 3)
-    v_step(6, 0)
     y2_step(1)
-    y2_step(3)
+    y2_step(0)
     z2_step(0)
     z3_step()
     x1_arrived(7)
     v_step(7, 1)
-    y2_step(0)
     v_step(7, 0)
     y3_step()
+    finish(v_acc[1], v2r.at[1], r2sem.at[3], 384)
     finish(z_acc[0:SUB], z3r, r3sem.at[0], 0)
+    finish(v_acc[0], v2r.at[0], r2sem.at[2], 256)
     finish(y_acc[Z - 1], y3r, r3sem.at[1], 128)
-    finish(v_acc[0], v2r.at[0], r2sem.at[2], 256)
-    finish(v_acc[1], v2r.at[1], r2sem.at[3], 384)
-
-    g_swap(core).wait_send()
+
+    drain(g_buf.at[pl.ds(0, TOK), :], gsend)
 
     drain(a_buf.at[:, pl.ds(0, TOK), :], asend)
     for buf, sem in (
@@ -459,7 +491,7 @@
         vm(Y - 1, SUB, 128), vm(Y - 1, SUB, 128),
         vm(Z - 1, SUB, 128), vm(Z - 1, SUB, 128),
         vm(BLOCK, 128, dtype=F32), vm(Z, SUB, 128, dtype=F32), vm(2, SUB, 128, dtype=F32),
-        dma, dma, dma, dma((Z,)), dma, dma,
+        dma, dma, dma, dma((Z + X - 1,)), dma, dma((2,)),
         dma, dma((24,)), dma, dma((24,)),
         dma, dma((Z,)), dma, dma((Z,)), dma, dma, dma((14,)),
         dma((4,)), dma((4,)), dma((2,)), dma((2,)),

time: 46.7 us -> 46.4 us (level)
  no operation moved by 1% of the time
where the time goes in v5:
time: 46.4 us; the launch traced here: 46.2 us
  Pallas kernels  44.8 us (97%)
  local copies, waits for them, and re-layouts  1.38 us (3%)
    pallas_call x1, Pallas kernels, per_device(): pl.pallas_call(kernel, out_shape=jax.ShapeDtypeStruct((SUB, COLS), F32),...  44.8 us
    unnamed x1, local copies, waits for them, and re-layouts  1.38 us

profile of v5, /device:TPU:8, one launch (start us, length us, event | category | flops | bytes accessed | tf_op | source)
XLA Modules:
  0.0 46.2 jit_solution(12406170433070817817)
XLA Ops:
  0.0 44.8 %shard_map.28 = f32[16,512]{1,0:T(8,128)} custom-call(bf16[256,8192]{1,0:T(8,128)(2,1)} %act_ref.1, bf16[256,512]{1,0:T(8,128)(2,1)} %grad_ref.1), custom_call_target="tpu_custom_call" | custom-call | flops 2684354560 | bytes 4456448 | tf_op jit(solution)/shard_map/pallas_call | solution.py:499
  44.9 1.4 %copy.4 = f32[16,512]{1,0:T(8,128)} copy(f32[16,512]{1,0:T(8,128)} %shard_map.28) | data formatting | bytes 65536

commit v6 on v5

--- a/solution.py
+++ b/solution.py
@@ -498,12 +498,12 @@
     ]
     return pl.pallas_call(
         kernel,
-        out_shape=jax.ShapeDtypeStruct((SUB, COLS), F32),
+        out_shape=pltpu.VMEM((SUB, COLS), F32),
         in_specs=[pl.BlockSpec(memory_space=pl.ANY)] * 2,
         out_specs=pl.BlockSpec(memory_space=pltpu.VMEM),
         scratch_shapes=scratch,
         compiler_params=pltpu.CompilerParams(
-            collective_id=0, has_side_effects=True, vmem_limit_bytes=60 * 1024 * 1024
+            collective_id=0, has_side_effects=True, vmem_limit_bytes=56 * 1024 * 1024
         ),
         cost_estimate=pl.CostEstimate(
             flops=2 * CORES * TOK * Z * WIDTH * (COLS + BLOCK),

time: 46.4 us -> 45 us (0.970)
  local copies, waits for them, and re-layouts: 1.38 us -> 0.62 us
  Pallas kernels: 44.8 us -> 44.2 us
    unnamed x1, local copies, waits for them, and re-layouts: 1.38 us -> 0.62 us
    pallas_call x1, Pallas kernels: 44.8 us -> 44.2 us  [per_device(): pl.pallas_call(kernel, out_shape=pltpu.VMEM((SUB, COLS), F32), in_specs=[...]
where the time goes in v6:
time: 45 us; the launch traced here: 44.9 us
  Pallas kernels  44.2 us (98%)
  local copies, waits for them, and re-layouts  0.62 us (1%)
    pallas_call x1, Pallas kernels, per_device(): pl.pallas_call(kernel, out_shape=pltpu.VMEM((SUB, COLS), F32), in_specs=[...  44.2 us

profile of v6, /device:TPU:8, one launch (start us, length us, event | category | flops | bytes accessed | tf_op | source)
XLA Modules:
  0.0 44.9 jit_solution(1799945738638946077)
XLA Ops:
  0.0 44.2 %shard_map.28 = f32[16,512]{1,0:T(8,128)S(1)} custom-call(bf16[256,8192]{1,0:T(8,128)(2,1)} %act_ref.1, bf16[256,512]{1,0:T(8,128)(2,1)} %grad_ref.1), custom_call_target="tpu_custom_call" | custom-call | flops 2684354560 | bytes 4456448 | tf_op jit(solution)/shard_map/pallas_call | solution.py:499
  44.3 0.6 %copy.4 = f32[16,512]{1,0:T(8,128)} copy(f32[16,512]{1,0:T(8,128)S(1)} %shard_map.28) | data formatting | bytes 65536

commit v7 on v6

--- a/solution.py
+++ b/solution.py
@@ -210,9 +210,9 @@
             at_x(way_sign(way)),
         )
 
-    def x1_copy(way, i):
-        return remote(
-            xs1.at[i, way], xr1.at[i, way], x1ssem, x1rsem.at[i],
+    def x1_copy(way, i, h):
+        return remote(
+            xs1.at[i, h, way], xr1.at[i, h, way], x1ssem, x1rsem.at[i, h],
             at_x(way_sign(way)),
         )
 
@@ -239,23 +239,26 @@
 
     def x1_step(i):
         drain(xr0.at[i], x0rsem.at[i])
-        for way in range(2):
-            j = 1 + 2 * way
-            mine = slice(way * HALF, (way + 1) * HALF)
-            rest = slice((1 - way) * HALF, (2 - way) * HALF)
-            xs1[i, way, mine] = (m_buf[i, j, mine, 256:512] + xr0[i, way].astype(F32)).astype(BF16)
-            xs1[i, way, rest] = m_buf[i, j, rest, 256:512].astype(BF16)
-            x1_copy(way, i).start()
+        for h in range(2):
+            there = slice(256 + h * 128, 384 + h * 128)
+            for way in range(2):
+                j = 1 + 2 * way
+                mine = slice(way * HALF, (way + 1) * HALF)
+                rest = slice((1 - way) * HALF, (2 - way) * HALF)
+                came = xr0[i, way, :, h * 128 : (h + 1) * 128].astype(F32)
+                xs1[i, h, way, mine] = (m_buf[i, j, mine, there] + came).astype(BF16)
+                xs1[i, h, way, rest] = m_buf[i, j, rest, there].astype(BF16)
+                x1_copy(way, i, h).start()
 
     def x2_rows(i, rows, h):
-        there = slice(h * 128, (h + 1) * 128)
         return (
             m_buf[i, 0, rows, 256 + h * 128 : 384 + h * 128]
-            + xr1[i, 0, rows, there].astype(F32)
-            + xr1[i, 1, rows, there].astype(F32)
+            + xr1[i, h, 0, rows].astype(F32)
+            + xr1[i, h, 1, rows].astype(F32)
         )
 
     def v_step(i, h):
+        drain(xr1.at[i, h], x1rsem.at[i, h])
         if i == 0:
             for way in range(2):
                 rows = slice(way * HALF, (way + 1) * HALF)
@@ -286,9 +289,6 @@
         for j in OFFSET[:-1]:
             v2s[h, j - 1] = part[j * SUB : (j + 1) * SUB].astype(BF16)
             w_copy(j, h).start()
-
-    def x1_arrived(i):
-        drain(xr1.at[i], x1rsem.at[i])
 
     def z2_step(j):
         drain(zr.at[pl.ds(slot(0, j, 3), 2)], zrsem.at[mark(0, j, 3)])
@@ -377,7 +377,6 @@
     z_step(0, 3, 1)
     y_step(0, 3, 1)
     x1_step(4)
-    x1_arrived(0)
     v_step(0, 1)
     v_step(0, 0)
     x0_step(7)
@@ -398,9 +397,7 @@
     x1_step(6)
     z_step(1, 3, 2)
     y_step(1, 0, 2)
-    x1_arrived(2)
     v_step(2, 1)
-    x1_arrived(1)
     v_step(1, 0)
     y_step(1, 2, 2)
     v_step(1, 1)
@@ -420,10 +417,8 @@
     z_step(1, 3, 3)
     y_step(0, 2, 3)
     x1_step(7)
-    x1_arrived(4)
     v_step(4, 1)
     y_step(1, 2, 3)
-    x1_arrived(3)
     v_step(3, 1)
     v_step(3, 0)
     y_step(0, 3, 3)
@@ -437,10 +432,8 @@
     y_step(0, 0, 3)
     z_step(0, 0, 3)
     z2_step(3)
-    x1_arrived(6)
     v_step(6, 1)
     y2_step(2)
-    x1_arrived(5)
     v_step(5, 1)
     v_step(6, 0)
     y2_step(3)
@@ -449,7 +442,6 @@
     y2_step(0)
     z2_step(0)
     z3_step()
-    x1_arrived(7)
     v_step(7, 1)
     v_step(7, 0)
     y3_step()
@@ -482,7 +474,7 @@
         vm(28, BLOCK, 128), vm(28, BLOCK, 128),
         vm(28, Z, SUB, 128), vm(28, Z, SUB, 128),
         vm(Z, 2, HALF, 256), vm(Z, 2, HALF, 256),
-        vm(Z, 2, BLOCK, 256), vm(Z, 2, BLOCK, 256),
+        vm(Z, 2, 2, BLOCK, 128), vm(Z, 2, 2, BLOCK, 128),
         vm(2, 2, HALF, 128), vm(2, 2, HALF, 128),
         vm(12, BLOCK, 128), vm(12, BLOCK, 128),
         vm(X - 1, BLOCK, 128), vm(X - 1, BLOCK, 128),
@@ -493,7 +485,7 @@
         vm(BLOCK, 128, dtype=F32), vm(Z, SUB, 128, dtype=F32), vm(2, SUB, 128, dtype=F32),
         dma, dma, dma, dma((Z + X - 1,)), dma, dma((2,)),
         dma, dma((24,)), dma, dma((24,)),
-        dma, dma((Z,)), dma, dma((Z,)), dma, dma, dma((14,)),
+        dma, dma((Z,)), dma, dma((Z, 2)), dma, dma, dma((14,)),
         dma((4,)), dma((4,)), dma((2,)), dma((2,)),
     ]
     return pl.pallas_call(

time: 45 us -> 45.1 us (level)
  no operation moved by 1% of the time
where the time goes in v7:
time: 45.1 us; the launch traced here: 45 us
  Pallas kernels  44.4 us (98%)
  local copies, waits for them, and re-layouts  0.62 us (1%)
    pallas_call x1, Pallas kernels, per_device(): pl.pallas_call(kernel, out_shape=pltpu.VMEM((SUB, COLS), F32), in_specs=[...  44.4 us

profile of v7, /device:TPU:8, one launch (start us, length us, event | category | flops | bytes accessed | tf_op | source)
XLA Modules:
  0.0 45.0 jit_solution(11662255495327814100)
XLA Ops:
  0.0 44.4 %shard_map.28 = f32[16,512]{1,0:T(8,128)S(1)} custom-call(bf16[256,8192]{1,0:T(8,128)(2,1)} %act_ref.1, bf16[256,512]{1,0:T(8,128)(2,1)} %grad_ref.1), custom_call_target="tpu_custom_call" | custom-call | flops 2684354560 | bytes 4456448 | tf_op jit(solution)/shard_map/pallas_call | solution.py:491
  44.4 0.6 %copy.4 = f32[16,512]{1,0:T(8,128)} copy(f32[16,512]{1,0:T(8,128)S(1)} %shard_map.28) | data formatting | bytes 65536
